TPU v7x, 128 devices: a whole 4x4x4 slice. The times are simulated.
128 devices in a mesh: comp: 4 (over x), tx: 4 (over y_hi, core), ty: 8 (over y_lo, z).
Axes of the slice: x: 4, y: 4 (y_hi: 2, y_lo: 2; y = y_hi * 2 + y_lo), z: 4, core: 2. Of those that a mesh axis runs over, the one named last changes fastest.
Arguments:
- model_state: float32 [4, 4, 8, 512, 2048], P('comp', None, None, 'tx', 'ty'), may hold values from -6 to 6
- sea_mask: int32 [4, 512, 2048], P('comp', 'tx', 'ty'), may hold values 0 or 1
- wave_speed: float32 [4, 8], P('comp'), may hold values from 0.1 to 0.4
- diffusivity: float32 [4, 8], P('comp'), may hold values from 0.02 to 0.2
- surface_gains: float32 [4, 3], P('comp'), may hold values from 0.1 to 0.5
- area_table: float32 [256], replicated, may hold values from 0.2 to 1
- own_cells: int32 [4, 32, 4, 2048], P('comp', ('tx', 'ty')), may hold values from 0 to 32767
- target_cells: int32 [4, 32, 4, 2048], P('comp', ('tx', 'ty')), may hold values from 0 to 32767
- weight_ids: int32 [4, 32, 4, 2048], P('comp', ('tx', 'ty')), may hold values from 0 to 255
- pair_counts: int32 [4, 32, 4], P('comp', ('tx', 'ty')), may hold values from 512 to 2048, as said below
- fold_map: int32 [512], replicated, may hold values from 0 to 511, as said below
Outputs:
- new_state: float32 [4, 4, 8, 512, 2048], P('comp', None, None, 'tx', 'ty')
Inputs may be any that keep to these rules, and one draw needn't show every extreme that they name: pair_counts[g, s, n] counts the live slots that position s of component g sends to its partner n; in every component one receiving position gets 2048 from each of the positions that have it as a partner. fold_map[fold_map[x]] == x.
All inputs are finite; a program needn't handle non-finite values. No bound on the sum of `sea_mask` on one device may be relied on, other than what follows from the above.
Results may differ from a plain program's by a relative error of at most 0.0001.
Values sent between devices are 32-bit elements; how exact they have to be, the bound alone decides.
A program may use at most 192 MiB of HBM per device.

v0:
```python
import jax
import jax.numpy as jnp
from jax import lax
from jax.sharding import PartitionSpec as P


def with_halo(array, sides, width):
    for axis, dim in sides:
        size, length = (lax.axis_size(axis), array.shape[dim])
        up = [(i, (i + 1) % size) for i in range(size)]
        down = [(j, i) for i, j in up]
        last = lax.slice_in_dim(array, length - width, length, axis=dim)
        first = lax.slice_in_dim(array, 0, width, axis=dim)
        before = lax.ppermute(last, axis, up)
        after = lax.ppermute(first, axis, down)
        array = jnp.concatenate([before, array, after], axis=dim)
    return array


def passed_along(block, axis, distance):
    devices = range(lax.axis_size(axis))
    route = [((i - distance) % len(devices), i) for i in devices]
    return lax.ppermute(block, axis, route)


def pick_cells(surface, cells, tile_rows, tile_cols):
    row_ids = jnp.arange(tile_rows, dtype=jnp.int32)
    col_ids = jnp.arange(tile_cols, dtype=jnp.int32)
    row_table = (cells[:, None] // tile_cols == row_ids[None, :]).astype(jnp.float32)
    col_table = (cells[:, None] % tile_cols == col_ids[None, :]).astype(jnp.float32)
    chosen_rows = jnp.einsum("kr,vrc->kvc", row_table, surface, precision=lax.Precision.HIGHEST)
    return jnp.einsum("kvc,kc->vk", chosen_rows, col_table, precision=lax.Precision.HIGHEST)


def add_cells(values, row_index, col_index, row_count, col_count):
    row_ids = jnp.arange(row_count, dtype=jnp.int32)
    col_ids = jnp.arange(col_count, dtype=jnp.int32)
    row_table = (row_index[:, None] == row_ids[None, :]).astype(jnp.float32)
    col_table = (col_index[:, None] == col_ids[None, :]).astype(jnp.float32)
    weighted = row_table[:, None, :] * jnp.transpose(values)[:, :, None]
    return jnp.einsum("kvr,kc->vrc", weighted, col_table, precision=lax.Precision.HIGHEST)


def extend_edges(fields, parity, fold_map, is_ocean):
    count_x = lax.axis_size("tx")
    count_y = lax.axis_size("ty")
    index_x = lax.axis_index("tx")
    index_y = lax.axis_index("ty")
    tile_rows = fields.shape[2]
    tile_cols = fields.shape[3]
    padded = with_halo(fields, (("tx", 2), ("ty", 3)), 1)
    atmosphere = jnp.logical_not(is_ocean)
    west_side = jnp.logical_and(atmosphere, index_x == 0)
    east_side = jnp.logical_and(atmosphere, index_x == count_x - 1)
    padded = padded.at[:, :, 0, :].multiply(jnp.where(west_side, 0.0, 1.0))
    padded = padded.at[:, :, tile_rows + 1, :].multiply(jnp.where(east_side, 0.0, 1.0))
    padded = padded.at[:, :, :, 0].multiply(jnp.where(index_y == 0, 0.0, 1.0))
    top_rows = fields[:, :, :, tile_cols - 1]
    whole_rows = lax.all_gather(top_rows, "tx", axis=2, tiled=True)
    partner = lax.dynamic_slice_in_dim(fold_map, index_x * tile_rows, tile_rows)
    folded = parity * jnp.take(whole_rows, partner, axis=2)
    northern = jnp.where(is_ocean, folded, jnp.zeros_like(folded))
    north_now = padded[:, :, 1 : tile_rows + 1, tile_cols + 1]
    chosen = jnp.where(index_y == count_y - 1, northern, north_now)
    return padded.at[:, :, 1 : tile_rows + 1, tile_cols + 1].set(chosen)


def shards(
    model_state,
    sea_mask,
    wave_speed,
    diffusivity,
    surface_gains,
    area_table,
    own_cells,
    target_cells,
    weight_ids,
    pair_counts,
    fold_map,
):
    comp_count = lax.axis_size("comp")
    row_step = lax.axis_size("ty")
    is_ocean = lax.axis_index("comp") == comp_count - 1
    fields = model_state[0]
    levels = fields.shape[1]
    tile_rows = fields.shape[2]
    tile_cols = fields.shape[3]
    sea_cells = sea_mask[0].astype(jnp.float32)
    near_count = own_cells.shape[2]
    slot_count = own_cells.shape[-1]
    slot_ids = jnp.arange(slot_count, dtype=jnp.int32)
    living = slot_ids[None, :] < pair_counts[0, 0][:, None]
    weight = jnp.where(living, area_table[weight_ids[0, 0]], 0.0)
    surface = fields[:, 0]
    picked = pick_cells(surface, own_cells[0, 0].reshape(-1), tile_rows, tile_cols).reshape(
        4, near_count, slot_count
    )
    slab = jnp.stack(
        [
            weight * picked[3],
            weight * picked[1],
            weight * picked[2],
            weight,
            target_cells[0, 0].astype(jnp.float32),
        ],
        axis=1,
    )
    arrived = [slab[0]]
    for partner in range(1, near_count):
        offset = partner % 2 + partner // 2 * row_step
        arrived.append(passed_along(slab[partner], ("tx", "ty"), offset))
    arrived = jnp.stack(arrived)
    receiver = jnp.where(is_ocean, slot_ids % (comp_count - 1), comp_count - 1)
    groups = jnp.arange(comp_count, dtype=jnp.int32)
    heading = (receiver[None, :] == groups[:, None])[:, None, None, :]
    routed = jnp.where(heading, arrived[None], 0.0)
    received = lax.all_to_all(routed, "comp", split_axis=0, concat_axis=0, tiled=True)

    def add_block(total, block):
        cells = block[:, 4].astype(jnp.int32).reshape(-1)
        values = jnp.moveaxis(block[:, :4], 1, 0).reshape(4, -1)
        return (
            total + add_cells(values, cells // tile_cols, cells % tile_cols, tile_rows, tile_cols),
            None,
        )

    start = jnp.zeros((4, tile_rows, tile_cols), jnp.float32)
    fluxes, unused = lax.scan(add_block, start, received)
    pressure, zonal, meridional, tracer = (fields[0], fields[1], fields[2], fields[3])
    first_level = (jnp.arange(levels, dtype=jnp.int32) == 0)[:, None, None]
    atmos_keep = jnp.where(first_level, 1.0 - surface_gains[0, 2] * (1.0 - sea_cells), 1.0)
    keeping = jnp.where(is_ocean, jnp.broadcast_to(sea_cells, atmos_keep.shape), atmos_keep)
    tendency_mask = jnp.where(is_ocean, sea_cells, 1.0)
    wave_factor = wave_speed[0][:, None, None]
    spread = diffusivity[0][:, None, None]
    scalars = extend_edges(jnp.stack([pressure, tracer]), 1.0, fold_map, is_ocean)
    pressure_pad, tracer_pad = (scalars[0], scalars[1])
    new_zonal = keeping * (
        zonal - 0.5 * wave_factor * (pressure_pad[:, 2:, 1:-1] - pressure_pad[:, :-2, 1:-1])
    )
    new_meridional = keeping * (
        meridional - 0.5 * wave_factor * (pressure_pad[:, 1:-1, 2:] - pressure_pad[:, 1:-1, :-2])
    )
    laplace = (
        tracer_pad[:, 2:, 1:-1]
        + tracer_pad[:, :-2, 1:-1]
        + tracer_pad[:, 1:-1, 2:]
        + tracer_pad[:, 1:-1, :-2]
        - 4.0 * tracer
    )
    new_tracer = tracer + spread * tendency_mask * laplace
    velocity = extend_edges(jnp.stack([new_zonal, new_meridional]), -1.0, fold_map, is_ocean)
    divergence = (
        velocity[0][:, 2:, 1:-1]
        - velocity[0][:, :-2, 1:-1]
        + velocity[1][:, 1:-1, 2:]
        - velocity[1][:, 1:-1, :-2]
    )
    new_pressure = pressure - 0.5 * wave_factor * divergence
    new_tracer = new_tracer.at[0].add(
        tendency_mask * surface_gains[0, 0] * (fluxes[0] - fluxes[3] * tracer[0])
    )
    new_zonal = new_zonal.at[0].add(
        tendency_mask * surface_gains[0, 1] * (fluxes[1] - fluxes[3] * zonal[0])
    )
    new_meridional = new_meridional.at[0].add(
        tendency_mask * surface_gains[0, 1] * (fluxes[2] - fluxes[3] * meridional[0])
    )
    return jnp.stack([new_pressure, new_zonal, new_meridional, new_tracer])[None]


def solution(mesh):
    in_specs = (
        P("comp", None, None, "tx", "ty"),
        P("comp", "tx", "ty"),
        P("comp", None),
        P("comp", None),
        P("comp", None),
        P(),
        P("comp", ("tx", "ty"), None, None),
        P("comp", ("tx", "ty"), None, None),
        P("comp", ("tx", "ty"), None, None),
        P("comp", ("tx", "ty"), None),
        P(),
    )
    out_specs = P("comp", None, None, "tx", "ty")
    return jax.shard_map(shards, mesh=mesh, in_specs=in_specs, out_specs=out_specs, check_vma=False)
```

profile of v0, /device:TPU:6, one launch (start us, length us, event | category | flops | bytes accessed | tf_op | source)
XLA Modules:
  0.0 809.6 jit_solution(8348266605255785786)
XLA Ops:
  0.0 1.8 slice_bitcast_fusion.1
  2.6 2.6 collective-permute-start.1
  6.1 4.7 copy.424
  12.4 51.2 %gather_fusion = f32[8192]{0:T(1024)S(1)} fusion(f32[256]{0:T(256)S(1)} %copy-done, s32[8192]{0:T(1024)S(1)} %broadcast_clamp_fusion), kind=kCustom, calls=%fused_computation.2 | custom fusion | bytes 98304 | tf_op jit(solution)/shard_map/gather | solution.py:93
  63.6 1.4 fusion.19
  65.1 18.2 %fusion.21 = f32[8192,4,256]{2,0,1:T(8,128)} fusion(s32[8192]{0:T(1024)S(1)} %get-tuple-element.234, f32[4,8,128,256]{3,2,0,1:T(8,128)} %bitcast.200), kind=kOutput, calls=%fused_computation.36 | convolution fusion | flops 12885950464 | bytes 34111488 | tf_op jit(solution)/shard_map/kr,vrc->kvc/dot_general | solution.py:31
  83.3 87.6 %fusion.16 = f32[8192,1,4]{2,1,0:T(1,128)} fusion(f32[8192,4,256]{2,0,1:T(8,128)} %fusion.21, pred[8192,256,1]{1,0,2:T(32,128)(4,1)S(1)} %fusion.19), kind=kOutput, calls=%fused_computation.27 | convolution fusion | flops 100663296 | bytes 35782656 | tf_op jit(solution)/shard_map/kvc,kc->vk/dot_general | solution.py:32
  170.9 7.9 copy.393
  182.2 2.0 collective-permute-start.10
  184.9 1.9 collective-permute-start.8
  189.0 1.5 pad_maximum_fusion.2
  193.3 1.2 multiply_subtract_fusion
  194.8 26.0 %copy.354 = f32[2,8,128,256]{1,0,2,3:T(2,128)} copy(f32[2,8,128,256]{3,2,1,0:T(8,128)} %pad_maximum_fusion.2) | data formatting | bytes 4194304 | tf_op jit(solution)/shard_map/stack | solution.py:136
  220.8 1.1 pad_maximum_fusion.10
  222.2 4.3 collective-permute-start.3
  226.4 6.7 all-gather
  235.0 116.2 %pad_maximum_fusion = f32[2,8,130,258]{1,0,2,3:T(2,128)} fusion(f32[2,8,130,1]{1,0,2,3:T(2,128)S(1)} %copy.358, f32[2,8,1,256]{1,0,2,3:T(2,128)S(1)} %collective-permute-done.1, f32[2,8,128,256]{1,0,2,3:T(2,128)} %copy.354, f32[2,8,1,256]{1,0,2,3:T(2,128)} %collective-permute-done, f32[2,8,130,1]{1,0,2,3:T(2,128)S(1)} %copy.357), kind=kLoop, calls=%fused_computation.25 | loop fusion | flops 2146560 | bytes 4293120 | tf_op jit(solution)/shard_map/concatenate | solution.py:16
  351.2 1.8 fusion.41
  353.0 1.9 fusion.40
  354.9 1.6 fusion.43
  356.5 1.8 fusion.55
  358.3 34.6 %fusion.77 = (f32[1,8,130,258]{1,0,2,3:T(1,128)}, f32[1,8,130,258]{1,0,2,3:T(1,128)}) fusion(f32[2,8,130,258]{1,0,2,3:T(2,128)} %fusion.55), kind=kLoop, calls=%fused_computation.173 | loop fusion | bytes 4293120 | tf_op jit(solution)/shard_map/slice | solution.py:137
  392.9 32.4 %copy.394 = f32[1,8,130,258]{3,2,1,0:T(8,128)} copy(f32[1,8,130,258]{1,0,2,3:T(1,128)} %get-tuple-element.210) | data formatting | bytes 2146560 | tf_op jit(solution)/shard_map/squeeze | solution.py:137
  425.3 4.7 fusion.37
  430.4 1.5 pad_maximum_fusion.3
  436.8 11.0 %all-gather.1 = f32[2,8,512,1]{2,1,3,0:T(8,128)S(1)} all-gather(f32[2,8,128,1]{2,1,3,0:T(8,128)S(1)} %copy.408), channel_id=3, replica_groups=mesh['comp'=4,'tx'=4,'ty'=8] {'tx'}, dimensions={2}, use_global_device_ids=true | all-gather | bytes 40960 | tf_op jit(solution)/shard_map/all_gather | solution.py:59
  448.8 32.4 %copy.402 = f32[1,8,130,258]{3,2,1,0:T(8,128)} copy(f32[1,8,130,258]{1,0,2,3:T(1,128)} %get-tuple-element.211) | data formatting | bytes 2146560 | tf_op jit(solution)/shard_map/squeeze | solution.py:137
  481.2 26.0 %copy.368 = f32[2,8,128,256]{1,0,2,3:T(2,128)} copy(f32[2,8,128,256]{3,2,1,0:T(8,128)} %pad_maximum_fusion.3) | data formatting | bytes 4194304 | tf_op jit(solution)/shard_map/stack | solution.py:152
  508.3 1.1 pad_maximum_fusion.7
  509.6 3.8 collective-permute-start.7
  513.4 1.0 broadcast_select_fusion
  514.4 4.8 all-to-all-start
  519.5 116.2 %pad_maximum_fusion.1 = f32[2,8,130,258]{1,0,2,3:T(2,128)} fusion(f32[2,8,130,1]{1,0,2,3:T(2,128)S(1)} %copy.372, f32[2,8,1,256]{1,0,2,3:T(2,128)S(1)} %collective-permute-done.5, f32[2,8,128,256]{1,0,2,3:T(2,128)} %copy.368, f32[2,8,1,256]{1,0,2,3:T(2,128)} %collective-permute-done.4, f32[2,8,130,1]{1,0,2,3:T(2,128)S(1)} %copy.371), kind=kLoop, calls=%fused_computation.26 | loop fusion | flops 2146560 | bytes 4293120 | tf_op jit(solution)/shard_map/concatenate | solution.py:16
  635.8 1.8 fusion.39
  637.6 1.9 fusion.38
  639.4 1.6 fusion.42
  641.0 1.8 fusion.52
  642.8 34.6 %fusion.76 = (f32[1,8,130,258]{1,0,2,3:T(1,128)}, f32[1,8,130,258]{1,0,2,3:T(1,128)}) fusion(f32[2,8,130,258]{1,0,2,3:T(2,128)} %fusion.52), kind=kLoop, calls=%fused_computation.172 | loop fusion | bytes 4293120 | tf_op jit(solution)/shard_map/slice | solution.py:154
  677.4 32.4 %copy.398 = f32[1,8,130,258]{3,2,1,0:T(8,128)} copy(f32[1,8,130,258]{1,0,2,3:T(1,128)} %get-tuple-element.208) | data formatting | bytes 2146560 | tf_op jit(solution)/shard_map/squeeze | solution.py:154
  709.7 32.3 %copy.400 = f32[1,8,130,258]{3,2,1,0:T(8,128)} copy(f32[1,8,130,258]{1,0,2,3:T(1,128)} %get-tuple-element.209) | data formatting | bytes 2146560 | tf_op jit(solution)/shard_map/squeeze | solution.py:156
  742.0 8.5 %fusion.31 = (f32[1,8,128,256]{3,2,1,0:T(8,128)}, f32[8,128,256]{2,1,0:T(8,128)S(1)}) fusion(f32[8,130,258]{2,1,0:T(8,128)} %bitcast.199, f32[8,130,258]{2,1,0:T(8,128)} %bitcast.198, f32[1,4,8,128,256]{4,3,2,1,0:T(8,128)} %param.37, f32[8]{0:T(128)S(1)} %copy-done.12, f32[8,130,258]{2,1,0:T(8,128)} %bitcast.196, f32[128,256]{1,0:T(8,128)S(1)} %copy-done.4, ...), kind=kLoop, calls=%fused_computation.63 | loop fusion | flops 3407872 | bytes 12714048 | tf_op jit(solution)/shard_map/stack | solution.py:169
  751.5 49.9 %while.24 = (s32[]{:T(128)}, f32[4,128,256]{2,1,0:T(8,128)}, f32[4,4,5,2048]{3,1,2,0:T(4,128)}, s32[]{:T(128)}, s32[]{:T(128)}) while((s32[]{:T(128)}, f32[4,128,256]{2,1,0:T(8,128)}, f32[4,4,5,2048]{3,1,2,0:T(4,128)}, s32[]{:T(128)}, s32[]{:T(128)}) %tuple.98), condition=%wide.region_1.3_spmd.clone, body=%wide.region_0.2_spmd.clone.sunk | while | flops 12893716480 | bytes 10715219 | solution.py:128
  753.2 10.1 %fusion.89 = f32[4,128,256]{2,1,0:T(8,128)} fusion(s32[8192]{0:T(1024)S(1)} %get-tuple-element.259, f32[8192,4]{0,1:T(4,128)S(1)} %bitcast.203, f32[8192,128]{0,1:T(8,128)S(1)} %fusion.88, f32[4,128,256]{2,1,0:T(8,128)} %get-tuple-element.267, pred[]{:T(512)S(6)} %compare.86), kind=kOutput, calls=%fused_computation.12.clone.1 | convolution fusion | flops 12891455488 | bytes 5406721 | tf_op jit(solution)/shard_map/while/body/eval_jaxpr/kvr,kc->vrc/dot_general | solution.py:41
  764.9 11.1 %fusion.89 = f32[4,128,256]{2,1,0:T(8,128)} fusion(s32[8192]{0:T(1024)S(1)} %get-tuple-element.259, f32[8192,4]{0,1:T(4,128)S(1)} %bitcast.203, f32[8192,128]{0,1:T(8,128)S(1)} %fusion.88, f32[4,128,256]{2,1,0:T(8,128)} %get-tuple-element.267, pred[]{:T(512)S(6)} %compare.86), kind=kOutput, calls=%fused_computation.12.clone.1 | convolution fusion | flops 12891455488 | bytes 5406721 | tf_op jit(solution)/shard_map/while/body/eval_jaxpr/kvr,kc->vrc/dot_general | solution.py:41
  777.6 11.1 %fusion.89 = f32[4,128,256]{2,1,0:T(8,128)} fusion(s32[8192]{0:T(1024)S(1)} %get-tuple-element.259, f32[8192,4]{0,1:T(4,128)S(1)} %bitcast.203, f32[8192,128]{0,1:T(8,128)S(1)} %fusion.88, f32[4,128,256]{2,1,0:T(8,128)} %get-tuple-element.267, pred[]{:T(512)S(6)} %compare.86), kind=kOutput, calls=%fused_computation.12.clone.1 | convolution fusion | flops 12891455488 | bytes 5406721 | tf_op jit(solution)/shard_map/while/body/eval_jaxpr/kvr,kc->vrc/dot_general | solution.py:41
  790.3 11.1 %fusion.89 = f32[4,128,256]{2,1,0:T(8,128)} fusion(s32[8192]{0:T(1024)S(1)} %get-tuple-element.259, f32[8192,4]{0,1:T(4,128)S(1)} %bitcast.203, f32[8192,128]{0,1:T(8,128)S(1)} %fusion.88, f32[4,128,256]{2,1,0:T(8,128)} %get-tuple-element.267, pred[]{:T(512)S(6)} %compare.86), kind=kOutput, calls=%fused_computation.12.clone.1 | convolution fusion | flops 12891455488 | bytes 5406721 | tf_op jit(solution)/shard_map/while/body/eval_jaxpr/kvr,kc->vrc/dot_general | solution.py:41
  801.4 3.3 fusion.49
  804.7 4.6 maximum_bitcast_fusion
  (133 shorter events, 29.5 us)
Async XLA Ops:
  0.0 12.3 %copy-start = (f32[256]{0:T(256)S(1)}, f32[256]{0:T(256)}, u32[]{:S(2)}) copy-start(f32[256]{0:T(256)} %param.42) | copy-start | bytes 3076
  2.6 218.2 %collective-permute-start.1 = (f32[2,8,1,256]{1,0,2,3:T(2,128)}, f32[2,8,1,256]{1,0,2,3:T(2,128)S(1)}, u32[]{:S(2)}, u32[]{:S(2)}) collective-permute-start(f32[2,8,1,256]{1,0,2,3:T(2,128)} %copy.353), channel_id=1, source_target_pairs={{8,0},{16,8},{24,16},{0,24},{9,1},{17,9},{25,17},{1,25},{10,2},{18... | collective-permute-start | bytes 49160 | tf_op jit(solution)/shard_map/ppermute | solution.py:15
  6.1 214.7 %collective-permute-start = (f32[2,8,1,256]{1,0,2,3:T(2,128)}, f32[2,8,1,256]{1,0,2,3:T(2,128)}, u32[]{:S(2)}, u32[]{:S(2)}) collective-permute-start(f32[2,8,1,256]{1,0,2,3:T(2,128)} %copy.352), channel_id=1, source_target_pairs={{0,8},{8,16},{16,24},{24,0},{1,9},{9,17},{17,25},{25,1},{2,10},{10... | collective-permute-start | bytes 49160 | tf_op jit(solution)/shard_map/ppermute | solution.py:14
  83.3 95.9 %copy-start.10 = (s32[1,1,4]{2,1,0:T(1,128)S(1)}, s32[1,1,4]{2,1,0:T(1,128)}, u32[]{:S(2)}) copy-start(s32[1,1,4]{2,1,0:T(1,128)} %param.46) | copy-start | bytes 52
  83.3 96.2 %copy-start.9 = (s32[1,1,4,2048]{3,2,1,0:T(4,128)S(1)}, s32[1,1,4,2048]{3,2,1,0:T(4,128)}, u32[]{:S(2)}) copy-start(s32[1,1,4,2048]{3,2,1,0:T(4,128)} %param.44) | copy-start | bytes 98308
  83.3 104.1 %copy-start.2 = (s32[1,128,256]{2,1,0:T(8,128)S(1)}, s32[1,128,256]{2,1,0:T(8,128)}, u32[]{:S(2)}) copy-start(s32[1,128,256]{2,1,0:T(8,128)} %param.38) | copy-start | bytes 393220
  83.3 107.3 %copy-start.14 = (f32[1,8]{1,0:T(1,128)S(1)}, f32[1,8]{1,0:T(1,128)}, u32[]{:S(2)}) copy-start(f32[1,8]{1,0:T(1,128)} %param.39) | copy-start | bytes 100
  83.3 107.8 %copy-start.11 = (f32[1,3]{1,0:T(1,128)S(1)}, f32[1,3]{1,0:T(1,128)}, u32[]{:S(2)}) copy-start(f32[1,3]{1,0:T(1,128)} %param.41) | copy-start | bytes 40
  180.9 326.3 %collective-permute-start.9 = (f32[5,2048]{1,0:T(8,128)}, f32[5,2048]{1,0:T(8,128)}, u32[]{:S(2)}, u32[]{:S(2)}) collective-permute-start(f32[5,2048]{1,0:T(8,128)} %bitcast.173), channel_id=1, source_target_pairs={{24,0},{25,1},{26,2},{27,3},{28,4},{29,5},{30,6},{31,7},{0,8},{1,9... | collective-permute-start | bytes 122888 | tf_op jit(solution)/shard_map/ppermute | solution.py:23
  182.2 325.0 %collective-permute-start.10 = (f32[5,2048]{1,0:T(8,128)}, f32[5,2048]{1,0:T(8,128)}, u32[]{:S(2)}, u32[]{:S(2)}) collective-permute-start(f32[5,2048]{1,0:T(8,128)} %bitcast.175), channel_id=1, source_target_pairs={{23,0},{24,1},{25,2},{26,3},{27,4},{28,5},{29,6},{30,7},{31,8},{0,... | collective-permute-start | bytes 122888 | tf_op jit(solution)/shard_map/ppermute | solution.py:23
  184.9 322.3 %collective-permute-start.8 = (f32[5,2048]{1,0:T(8,128)}, f32[5,2048]{1,0:T(8,128)}, u32[]{:S(2)}, u32[]{:S(2)}) collective-permute-start(f32[5,2048]{1,0:T(8,128)} %bitcast.174), channel_id=1, source_target_pairs={{31,0},{0,1},{1,2},{2,3},{3,4},{4,5},{5,6},{6,7},{7,8},{8,9},{9,10... | collective-permute-start | bytes 122888 | tf_op jit(solution)/shard_map/ppermute | solution.py:23
  220.8 12.6 %copy-start.8 = (f32[1,5,2048]{2,0,1:T(1,128)S(1)}, f32[1,5,2048]{2,0,1:T(1,128)}, u32[]{:S(2)}) copy-start(f32[1,5,2048]{2,0,1:T(1,128)} %get-tuple-element.229) | copy-start | bytes 122884
  222.2 12.7 %collective-permute-start.3 = (f32[2,8,130,1]{2,1,3,0:T(8,128)S(1)}, f32[2,8,130,1]{2,1,3,0:T(8,128)S(1)}, u32[]{:S(2)}, u32[]{:S(2)}) collective-permute-start(f32[2,8,130,1]{2,1,3,0:T(8,128)S(1)} %copy.356), channel_id=1, source_target_pairs={{1,0},{2,1},{3,2},{4,3},{5,4},{6,5},{7,6},{0,7},{9,8},{10,9},{11,1... | collective-permute-start | bytes 24968 | tf_op jit(solution)/shard_map/ppermute | solution.py:15
  226.4 8.3 %collective-permute-start.2 = (f32[2,8,130,1]{2,1,3,0:T(8,128)S(1)}, f32[2,8,130,1]{2,1,3,0:T(8,128)S(1)}, u32[]{:S(2)}, u32[]{:S(2)}) collective-permute-start(f32[2,8,130,1]{2,1,3,0:T(8,128)S(1)} %copy.355), channel_id=1, source_target_pairs={{0,1},{1,2},{2,3},{3,4},{4,5},{5,6},{6,7},{7,0},{8,9},{9,10},{10,1... | collective-permute-start | bytes 24968 | tf_op jit(solution)/shard_map/ppermute | solution.py:14
  392.9 32.4 %copy-start.5 = (f32[128,256]{1,0:T(8,128)S(1)}, f32[128,256]{1,0:T(8,128)}, u32[]{:S(2)}) copy-start(f32[128,256]{1,0:T(8,128)} %convert_bitcast_fusion) | copy-start | bytes 393220
  392.9 32.4 %copy-start.6 = (f32[128,256]{1,0:T(8,128)S(1)}, f32[128,256]{1,0:T(8,128)}, u32[]{:S(2)}) copy-start(f32[128,256]{1,0:T(8,128)} %multiply_subtract_fusion) | copy-start | bytes 393220
  392.9 32.4 %copy-start.12 = (f32[8]{0:T(128)S(1)}, f32[8]{0:T(128)}, u32[]{:S(2)}) copy-start(f32[8]{0:T(128)} %multiply_bitcast_fusion) | copy-start | bytes 100
  435.6 72.7 %collective-permute-start.5 = (f32[2,8,1,256]{1,0,2,3:T(2,128)}, f32[2,8,1,256]{1,0,2,3:T(2,128)S(1)}, u32[]{:S(2)}, u32[]{:S(2)}) collective-permute-start(f32[2,8,1,256]{1,0,2,3:T(2,128)} %copy.367), channel_id=1, source_target_pairs={{8,0},{16,8},{24,16},{0,24},{9,1},{17,9},{25,17},{1,25},{10,2},{18... | collective-permute-start | bytes 49160 | tf_op jit(solution)/shard_map/ppermute | solution.py:15
  436.4 71.8 %collective-permute-start.4 = (f32[2,8,1,256]{1,0,2,3:T(2,128)}, f32[2,8,1,256]{1,0,2,3:T(2,128)}, u32[]{:S(2)}, u32[]{:S(2)}) collective-permute-start(f32[2,8,1,256]{1,0,2,3:T(2,128)} %copy.366), channel_id=1, source_target_pairs={{0,8},{8,16},{16,24},{24,0},{1,9},{9,17},{17,25},{25,1},{2,10},{10... | collective-permute-start | bytes 49160 | tf_op jit(solution)/shard_map/ppermute | solution.py:14
  481.2 26.0 %copy-start.7 = (f32[1,5,2048]{2,1,0:T(8,128)S(1)}, f32[1,5,2048]{2,1,0:T(8,128)}, u32[]{:S(2)}) copy-start(f32[1,5,2048]{2,1,0:T(8,128)} %copy.409) | copy-start | bytes 122884
  509.6 9.8 %collective-permute-start.7 = (f32[2,8,130,1]{2,1,3,0:T(8,128)S(1)}, f32[2,8,130,1]{2,1,3,0:T(8,128)S(1)}, u32[]{:S(2)}, u32[]{:S(2)}) collective-permute-start(f32[2,8,130,1]{2,1,3,0:T(8,128)S(1)} %copy.370), channel_id=1, source_target_pairs={{1,0},{2,1},{3,2},{4,3},{5,4},{6,5},{7,6},{0,7},{9,8},{10,9},{11,1... | collective-permute-start | bytes 24968 | tf_op jit(solution)/shard_map/ppermute | solution.py:15
  513.4 5.8 collective-permute-start.6
  514.4 237.0 %all-to-all-start = ((f32[4,4,5,2048]{3,1,2,0:T(4,128)}), f32[4,4,5,2048]{3,1,2,0:T(4,128)}, u32[]{:S(2)}, u32[]{:S(2)}) async-start(f32[4,4,5,2048]{3,1,2,0:T(4,128)} %broadcast_select_fusion), calls=%async_computation | async-start | bytes 1310720 | tf_op jit(solution)/shard_map/all_to_all | solution.py:117
  677.4 64.7 %copy-start.4 = (f32[128,256]{1,0:T(8,128)S(1)}, f32[128,256]{1,0:T(8,128)}, u32[]{:S(2)}) copy-start(f32[128,256]{1,0:T(8,128)} %fusion.63) | copy-start | bytes 393220
  677.4 64.7 %copy-start.13 = (f32[1,8]{1,0:T(1,128)S(1)}, f32[1,8]{1,0:T(1,128)}, u32[]{:S(2)}) copy-start(f32[1,8]{1,0:T(1,128)} %param.40) | copy-start | bytes 100
  751.5 49.9 %copy-start.3 = (s32[1,128,256]{2,1,0:T(8,128)S(1)}, s32[1,128,256]{2,1,0:T(8,128)}, u32[]{:S(2)}) copy-start(s32[1,128,256]{2,1,0:T(8,128)} %param.38) | copy-start | bytes 393220
  801.4 8.0 copy-start.1
where the time goes:
time: 823 us; the launch traced here: 810 us
  local copies, waits for them, and re-layouts  335 us (41%)
  other arithmetic  285 us (35%)
  matrix products  149 us (18%)
  starting transfers between devices  21 us (3%)
  blocking collectives  17.7 us (2%)
    concatenate x2, other arithmetic, with_halo(): array = jnp.concatenate([before, array, after], axis=dim)  232 us
    dot_general x1, matrix products, pick_cells(): jnp.einsum('kvc,kc->vk', chosen_rows, col_table, precision=lax.Precision....  87.6 us
    squeeze x2, local copies, waits for them, and re-layouts, shards(): pressure_pad, tracer_pad = (scalars[0], scalars[1])  64.8 us
    gather x2, local copies, waits for them, and re-layouts, shards(): weight = jnp.where(living, area_table[weight_ids[0, 0]], 0.0)  51.2 us
    dot_general x4, matrix products, add_cells(): jnp.einsum('kvr,kc->vrc', weighted, col_table, precision=lax.Precision.HI...  43.6 us
    slice x1, local copies, waits for them, and re-layouts, shards(): pressure_pad, tracer_pad = (scalars[0], scalars[1])  34.6 us
    slice x1, local copies, waits for them, and re-layouts, shards(): velocity[0][:, 2:, 1:-1] - velocity[0][:, :-2, 1:-1]  34.6 us
    squeeze x1, local copies, waits for them, and re-layouts, shards(): velocity[0][:, 2:, 1:-1] - velocity[0][:, :-2, 1:-1]  32.4 us
  transfers between devices with their start and end apart: 12, of which 0 were waited for; matrix products, arithmetic and copies ran while one was open for 87% of the time, Pallas kernels for 0%

commit v1 on v0

v1 whole, which is shorter than its diff:
```python
import jax
import jax.numpy as jnp
from jax import lax
from jax.experimental import pallas as pl
from jax.experimental.pallas import tpu as pltpu
from jax.sharding import PartitionSpec as P

MESH = pl.DeviceIdType.MESH
NEAR = 4
ROWS = 128
COLS = 256
GROUP = 8


def exchange_kernel(
    counts,
    state,
    mask,
    own,
    target,
    ids,
    cells_out,
    values_out,
    rows_out,
    columns_out,
    fold_out,
    fields,
    sea,
    own_v,
    target_v,
    ids_v,
    surface,
    early,
    late,
    rows_in,
    columns_in,
    load_sem,
    early_send,
    early_recv,
    late_send,
    late_recv,
    edge_send,
    edge_recv,
    fold_send,
    fold_recv,
):
    levels = fields.shape[1]
    comps = lax.axis_size("comp")
    windows = comps - 1
    count_x = lax.axis_size("tx")
    count_y = lax.axis_size("ty")
    places = count_x * count_y
    comp = lax.axis_index("comp")
    ix = lax.axis_index("tx")
    iy = lax.axis_index("ty")
    place = ix * count_y + iy
    is_ocean = comp == windows
    is_window = comp != windows
    on_fold = jnp.logical_and(is_ocean, iy == count_y - 1)
    offsets = [n % 2 + (n // 2) * count_y for n in range(NEAR)]

    def device_at(component, position):
        return (component, lax.div(position, count_y), lax.rem(position, count_y))

    loads = [
        pltpu.make_async_copy(own.at[0, 0], own_v, load_sem.at[0]),
        pltpu.make_async_copy(state.at[0, :, 0], fields.at[:, 0], load_sem.at[1]),
        pltpu.make_async_copy(target.at[0, 0], target_v, load_sem.at[2]),
        pltpu.make_async_copy(ids.at[0, 0], ids_v, load_sem.at[3]),
        pltpu.make_async_copy(
            state.at[0, :, pl.ds(1, levels - 1)], fields.at[:, pl.ds(1, levels - 1)], load_sem.at[4]
        ),
        pltpu.make_async_copy(mask.at[0], sea, load_sem.at[5]),
    ]
    for load in loads:
        load.start()

    west = (comp, lax.rem(ix + count_x - 1, count_x), iy)
    east = (comp, lax.rem(ix + 1, count_x), iy)
    south = (comp, ix, lax.rem(iy + count_y - 1, count_y))
    north = (comp, ix, lax.rem(iy + 1, count_y))

    barrier = pltpu.get_barrier_semaphore()
    for neighbour in (west, east, south, north):
        pl.semaphore_signal(barrier, inc=1, device_id=neighbour, device_id_type=MESH)
    sources = [lax.rem(place + places - offset, places) for offset in offsets]

    @pl.when(is_ocean)
    def _():
        for source in sources:
            for window in range(windows):
                pl.semaphore_signal(
                    barrier, inc=1, device_id=device_at(window, source), device_id_type=MESH
                )

    @pl.when(is_window)
    def _():
        for source in sources:
            pl.semaphore_signal(
                barrier, inc=1, device_id=device_at(windows, source), device_id_type=MESH
            )

    @pl.when(on_fold)
    def _():
        for step in range(1, count_x):
            pl.semaphore_signal(
                barrier,
                inc=1,
                device_id=(comp, lax.rem(ix + step, count_x), iy),
                device_id_type=MESH,
            )

    loads[2].wait()
    loads[3].wait()
    lane = lax.broadcasted_iota(jnp.int32, (1, COLS), 1)
    for n in range(NEAR):
        live = counts[0, 0, n]
        for row in range(GROUP):
            span = slice(row * COLS, (row + 1) * COLS)
            cell = target_v[n : n + 1, span]
            early[n, row : row + 1] = jnp.where(lane + row * COLS < live, cell, -1)
            early[n, GROUP + row : GROUP + row + 1] = ids_v[n : n + 1, span]

    @pl.when(is_window)
    def _():
        pl.semaphore_wait(barrier, 4 + NEAR)

    @pl.when(jnp.logical_and(is_ocean, iy != count_y - 1))
    def _():
        pl.semaphore_wait(barrier, 4 + windows * NEAR)

    @pl.when(on_fold)
    def _():
        pl.semaphore_wait(barrier, 4 + windows * NEAR + count_x - 1)

    slot = jnp.where(is_ocean, 0, comp * NEAR)

    def packet_copy(kind, n, window, component):
        position = lax.rem(place + offsets[n], places)
        source, target_ref, send, recv = {
            "early": (early, cells_out, early_send, early_recv),
            "late": (late, values_out, late_send, late_recv),
        }[kind]
        return pltpu.make_async_remote_copy(
            src_ref=source.at[n],
            dst_ref=target_ref.at[slot + n],
            send_sem=send.at[n * windows + window],
            recv_sem=recv.at[slot + n],
            device_id=device_at(component, position),
            device_id_type=MESH,
        )

    def send_packets(kind, n):
        @pl.when(is_ocean)
        def _():
            for window in range(windows):
                packet_copy(kind, n, window, window).start()

        @pl.when(is_window)
        def _():
            packet_copy(kind, n, 0, windows).start()

    for n in range(NEAR):
        send_packets("early", n)

    loads[0].wait()
    loads[1].wait()
    for at, variable in enumerate((3, 1, 2)):
        turned = jnp.transpose(fields[variable, 0])
        high = turned.astype(jnp.bfloat16)
        low = (turned - high.astype(jnp.float32)).astype(jnp.bfloat16)
        surface[at * COLS : (at + 1) * COLS, 0:ROWS] = high
        surface[at * COLS : (at + 1) * COLS, ROWS : 2 * ROWS] = low

    row_ids = lax.broadcasted_iota(jnp.int32, (ROWS, COLS), 0)
    col_ids = lax.broadcasted_iota(jnp.int32, (COLS, COLS), 0)

    def pick(n):
        def pick_row(row, carry):
            cell = own_v[n : n + 1, pl.ds(pl.multiple_of(row * COLS, COLS), COLS)]
            hot = jnp.where(row_ids == (cell >> 8), 1.0, 0.0).astype(jnp.bfloat16)
            chosen = jnp.dot(
                surface[...],
                jnp.concatenate([hot, hot], axis=0),
                preferred_element_type=jnp.float32,
            )
            here = col_ids == (cell & (COLS - 1))
            for at in range(3):
                part = jnp.where(here, chosen[at * COLS : (at + 1) * COLS], 0.0)
                late[n, pl.ds(at * GROUP + row, 1), :] = jnp.sum(part, axis=0, keepdims=True)
            return carry

        lax.fori_loop(0, GROUP, pick_row, 0, unroll=2)
        send_packets("late", n)

    edge_copies = []
    for at, device in enumerate((west, east)):
        edge_copies.append(
            pltpu.make_async_remote_copy(
                src_ref=rows_in.at[at],
                dst_ref=rows_out.at[1 - at],
                send_sem=edge_send.at[at],
                recv_sem=edge_recv.at[1 - at],
                device_id=device,
                device_id_type=MESH,
            )
        )
    for at, device in enumerate((south, north)):
        edge_copies.append(
            pltpu.make_async_remote_copy(
                src_ref=columns_in.at[at],
                dst_ref=columns_out.at[1 - at],
                send_sem=edge_send.at[2 + at],
                recv_sem=edge_recv.at[2 + 1 - at],
                device_id=device,
                device_id_type=MESH,
            )
        )

    def fold_copy(step):
        return pltpu.make_async_remote_copy(
            src_ref=columns_in.at[1],
            dst_ref=fold_out.at[ix],
            send_sem=fold_send.at[step],
            recv_sem=fold_recv.at[step],
            device_id=(comp, lax.rem(ix + step, count_x), iy),
            device_id_type=MESH,
        )

    fold_keep = pltpu.make_async_copy(columns_in.at[1], fold_out.at[ix], fold_send.at[0])

    def send_edges():
        loads[4].wait()
        loads[5].wait()
        for at, (near, far) in enumerate(((0, 1), (ROWS - 1, ROWS - 2))):
            for level in range(levels):
                for item, (variable, row) in enumerate(((0, near), (0, far), (1, near), (3, near))):
                    rows_in[at, item * 8 + level : item * 8 + level + 1] = fields[
                        variable, level, row : row + 1, :
                    ]
            rows_in[at, 32:33] = sea[near : near + 1].astype(jnp.float32)
        lanes = lax.broadcasted_iota(jnp.int32, (ROWS, 128), 1)
        for at, (near, far) in enumerate(((0, 1), (127, 126))):
            half = slice(at * 128, (at + 1) * 128)
            columns_in[at] = jnp.where(
                lanes == 32,
                pltpu.roll(sea[:, half].astype(jnp.float32), (32 - near) % 128, 1),
                0.0,
            )

            def add_level(level, carry):
                packed = columns_in[at]
                for item, (variable, column) in enumerate(
                    ((0, near), (0, far), (2, near), (3, near))
                ):
                    place_at = item * 8 + level
                    turned = pltpu.roll(
                        fields[variable, level, :, half],
                        lax.rem(place_at + (128 - column), 128),
                        1,
                    )
                    packed = jnp.where(lanes == place_at, turned, packed)
                columns_in[at] = packed
                return carry

            lax.fori_loop(0, levels, add_level, 0)
        for copy in edge_copies:
            copy.start()

        @pl.when(on_fold)
        def _():
            fold_keep.start()
            for step in range(1, count_x):
                fold_copy(step).start()

    pick(0)
    pick(1)
    send_edges()
    pick(2)
    pick(3)

    for copy in edge_copies:
        copy.wait_send()
        copy.wait_recv()

    @pl.when(on_fold)
    def _():
        fold_keep.wait()
        for step in range(1, count_x):
            fold_copy(step).wait_send()
            fold_copy(step).wait_recv()

    def wait_slot(kind, at):
        target_ref, recv, source = {
            "early": (cells_out, early_recv, early),
            "late": (values_out, late_recv, late),
        }[kind]
        pltpu.make_async_remote_copy(
            src_ref=source.at[0],
            dst_ref=target_ref.at[at],
            send_sem=early_send.at[0],
            recv_sem=recv.at[at],
            device_id=west,
            device_id_type=MESH,
        ).wait_recv()

    for kind in ("early", "late"):

        @pl.when(is_ocean)
        def _():
            for n in range(NEAR):
                for window in range(windows):
                    packet_copy(kind, n, window, window).wait_send()
            for at in range(windows * NEAR):
                wait_slot(kind, at)

        @pl.when(is_window)
        def _():
            for n in range(NEAR):
                packet_copy(kind, n, 0, windows).wait_send()
            for at in range(NEAR):
                wait_slot(kind, at)


def step_kernel(
    wave,
    spread,
    gains,
    state,
    mask,
    area,
    fold_map,
    cells,
    values,
    rows,
    columns,
    folded,
    result,
    fields,
    updated,
    land,
    area_v,
    fold_v,
    cells_v,
    values_v,
    rows_v,
    columns_v,
    folded_v,
    sea_v,
    row_of,
    col_of,
    addends,
    left,
    right,
    total,
    load_sem,
    level_sem,
    store_sem,
):
    levels = fields.shape[0]
    windows = lax.axis_size("comp") - 1
    count_x = lax.axis_size("tx")
    count_y = lax.axis_size("ty")
    comp = lax.axis_index("comp")
    ix = lax.axis_index("tx")
    iy = lax.axis_index("ty")
    is_ocean = comp == windows
    on_fold = jnp.logical_and(is_ocean, iy == count_y - 1)
    packets = cells_v.shape[0]

    def level_load(level):
        return pltpu.make_async_copy(state.at[0, :, level], fields.at[level], level_sem.at[level])

    def level_store(level):
        return pltpu.make_async_copy(
            updated.at[level], result.at[0, :, level], store_sem.at[level]
        )

    loads = [
        pltpu.make_async_copy(cells, cells_v, load_sem.at[0]),
        pltpu.make_async_copy(values, values_v, load_sem.at[1]),
        pltpu.make_async_copy(area, area_v, load_sem.at[2]),
        pltpu.make_async_copy(mask.at[0], sea_v, load_sem.at[3]),
        pltpu.make_async_copy(rows, rows_v, load_sem.at[4]),
        pltpu.make_async_copy(columns, columns_v, load_sem.at[5]),
        pltpu.make_async_copy(fold_map.at[pl.ds(ix * ROWS, ROWS)], fold_v, load_sem.at[6]),
    ]
    for load in loads:
        load.start()
    fold_load = pltpu.make_async_copy(folded, folded_v, load_sem.at[7])

    @pl.when(on_fold)
    def _():
        fold_load.start()

    for level in range(levels):
        level_load(level).start()
    for load in loads[:3]:
        load.wait()

    table = [
        jnp.broadcast_to(area_v[at * 128 : (at + 1) * 128][None], (GROUP, 128)) for at in range(2)
    ]
    slot_ids = lax.broadcasted_iota(
        jnp.int32, (GROUP, COLS), 0
    ) * COLS + lax.broadcasted_iota(jnp.int32, (GROUP, COLS), 1)
    mine = jnp.logical_or(slot_ids - 3 * ((slot_ids * 43691) >> 17) == comp, is_ocean)

    def prepare(at, carry):
        cell = cells_v[at, 0:GROUP]
        entry = cells_v[at, GROUP : 2 * GROUP]
        halves = []
        for half in range(2):
            index = entry[:, half * 128 : (half + 1) * 128]
            low = jnp.take_along_axis(table[0], index & 127, axis=1, mode="promise_in_bounds")
            high = jnp.take_along_axis(table[1], index & 127, axis=1, mode="promise_in_bounds")
            halves.append(jnp.where(index < 128, low, high))
        weight = jnp.concatenate(halves, axis=1)
        row = cell >> 8
        row_of[at] = row & 63
        alive = jnp.logical_and(cell >= 0, mine)
        col_of[at] = jnp.where(alive, ((row >> 6) << 8) + (cell & (COLS - 1)), -1)
        for item in range(4):
            value = weight
            if item < 3:
                value = weight * values_v[at, item * GROUP : (item + 1) * GROUP]
            high = value.astype(jnp.bfloat16).astype(jnp.float32)
            addends[at, 2 * item] = high
            addends[at, 2 * item + 1] = value - high
        return carry

    lax.fori_loop(0, jnp.where(is_ocean, packets, NEAR), prepare, 0)
    total[...] = jnp.zeros_like(total)

    for load in loads[3:]:
        load.wait()

    land[...] = 1.0 - sea_v[...].astype(jnp.float32)
    one = jnp.float32(1.0)
    zero = jnp.float32(0.0)
    valid_west = jnp.where(jnp.logical_or(is_ocean, ix > 0), one, zero)
    valid_east = jnp.where(jnp.logical_or(is_ocean, ix < count_x - 1), one, zero)
    valid_south = jnp.where(iy > 0, one, zero)
    valid_north = jnp.where(jnp.logical_or(is_ocean, iy < count_y - 1), one, zero)

    @pl.when(on_fold)
    def _():
        fold_load.wait()
        wanted = jnp.transpose(jnp.broadcast_to(fold_v[...][None], (ROWS, ROWS)))
        lanes = lax.broadcasted_iota(jnp.int32, (ROWS, 128), 1)
        gathered = jnp.zeros((ROWS, 128), jnp.float32)
        for block in range(count_x):
            hot = jnp.where(wanted == lanes + block * ROWS, 1.0, 0.0).astype(jnp.bfloat16)
            rest = folded_v[block]
            for part in range(3):
                piece = rest.astype(jnp.bfloat16)
                rest = rest - piece.astype(jnp.float32)
                gathered += jnp.dot(hot, piece, preferred_element_type=jnp.float32)
        turned = jnp.logical_and(lanes >= 16, lanes < 24)
        columns_v[1] = jnp.where(turned, -gathered, gathered)

    rows_v[0] = rows_v[0] * valid_west
    rows_v[1] = rows_v[1] * valid_east
    columns_v[0] = columns_v[0] * valid_south
    columns_v[1] = columns_v[1] * valid_north

    row_ids = lax.broadcasted_iota(jnp.int32, (ROWS, COLS), 0)
    col_ids = lax.broadcasted_iota(jnp.int32, (ROWS, COLS), 1)
    is_first_row = row_ids == 0
    is_last_row = row_ids == ROWS - 1
    is_first_col = col_ids == 0
    is_last_col = col_ids == COLS - 1
    ocean_share = jnp.where(is_ocean, one, zero)

    def before_x(field, edge):
        return jnp.where(is_first_row, edge, pltpu.roll(field, 1, 0))

    def after_x(field, edge):
        return jnp.where(is_last_row, edge, pltpu.roll(field, ROWS - 1, 0))

    def before_y(field, edge):
        return jnp.where(is_first_col, edge, pltpu.roll(field, 1, 1))

    def after_y(field, edge):
        return jnp.where(is_last_col, edge, pltpu.roll(field, COLS - 1, 1))

    def stencil(level):
        level_load(level).wait()
        pressure = fields[level, 0]
        zonal = fields[level, 1]
        meridional = fields[level, 2]
        tracer = fields[level, 3]
        half_wave = 0.5 * wave[0, level]
        drag = jnp.where(is_ocean, one, jnp.where(level == 0, gains[0, 2], zero))
        keeping = 1.0 - drag * land[...]
        tendency = 1.0 - ocean_share * land[...]
        edge_rows = [
            [rows_v[side, pl.ds(item * 8 + level, 1), :] for item in range(4)] for side in range(2)
        ]
        turn = lax.rem(128 - level, 128)
        shifted = [pltpu.roll(columns_v[side], turn, 1) for side in range(2)]
        edge_cols = [
            [shifted[side][:, item * 8 : item * 8 + 1] for item in range(4)] for side in range(2)
        ]
        row_keep = [
            (1.0 - drag * (1.0 - rows_v[0, 32:33, :])) * valid_west,
            (1.0 - drag * (1.0 - rows_v[1, 32:33, :])) * valid_east,
        ]
        col_keep = [
            (1.0 - drag * (1.0 - columns_v[0, :, 32:33])) * valid_south,
            (1.0 - drag * (1.0 - columns_v[1, :, 32:33])) * valid_north,
        ]
        new_zonal = keeping * (
            zonal
            - half_wave
            * (after_x(pressure, edge_rows[1][0]) - before_x(pressure, edge_rows[0][0]))
        )
        new_meridional = keeping * (
            meridional
            - half_wave
            * (after_y(pressure, edge_cols[1][0]) - before_y(pressure, edge_cols[0][0]))
        )
        zonal_west = row_keep[0] * (
            edge_rows[0][2] - half_wave * (pressure[0:1] - edge_rows[0][1])
        )
        zonal_east = row_keep[1] * (
            edge_rows[1][2] - half_wave * (edge_rows[1][1] - pressure[ROWS - 1 : ROWS])
        )
        meridional_south = col_keep[0] * (
            edge_cols[0][2] - half_wave * (pressure[:, 0:1] - edge_cols[0][1])
        )
        meridional_north = col_keep[1] * (
            edge_cols[1][2] - half_wave * (edge_cols[1][1] - pressure[:, COLS - 1 : COLS])
        )
        divergence = (
            after_x(new_zonal, zonal_east)
            - before_x(new_zonal, zonal_west)
            + after_y(new_meridional, meridional_north)
            - before_y(new_meridional, meridional_south)
        )
        laplace = (
            after_x(tracer, edge_rows[1][3])
            + before_x(tracer, edge_rows[0][3])
            + after_y(tracer, edge_cols[1][3])
            + before_y(tracer, edge_cols[0][3])
            - 4.0 * tracer
        )
        updated[level, 0] = pressure - half_wave * divergence
        updated[level, 1] = new_zonal
        updated[level, 2] = new_meridional
        updated[level, 3] = tracer + spread[0, level] * tendency * laplace

    narrow_ids = lax.broadcasted_iota(jnp.int32, (64, COLS), 0)
    wide_ids = lax.broadcasted_iota(jnp.int32, (2 * COLS, COLS), 0)

    def scatter(first, row):
        for at in range(4):
            span = slice(at * COLS, (at + 1) * COLS)
            here = narrow_ids == row_of[first + at, pl.ds(row, 1), :]
            for item in range(4):
                for part in range(2):
                    value = addends[first + at, 2 * item + part, pl.ds(row, 1), :]
                    lead = (part * 4 + item) * 64
                    left[lead : lead + 64, span] = jnp.where(here, value, 0.0).astype(jnp.bfloat16)
            there = wide_ids == col_of[first + at, pl.ds(row, 1), :]
            right[:, span] = jnp.where(there, 1.0, 0.0).astype(jnp.bfloat16)
        total[...] += lax.dot_general(
            left[...],
            right[...],
            (((1,), (1,)), ((), ())),
            preferred_element_type=jnp.float32,
        )

    def level_step(level, carry):
        stencil(level)
        scatter(0, level)

        @pl.when(is_ocean)
        def _():
            scatter(4, level)
            scatter(8, level)

        @pl.when(level > 0)
        def _():
            level_store(level).start()

        return carry

    lax.fori_loop(0, levels, level_step, 0)
    for row in range(levels, GROUP):
        scatter(0, row)

        @pl.when(is_ocean)
        def _():
            scatter(4, row)
            scatter(8, row)

    for half in range(2):
        span = slice(half * 64, (half + 1) * 64)
        lanes = slice(half * COLS, (half + 1) * COLS)
        sums = [
            total[item * 64 : (item + 1) * 64, lanes]
            + total[256 + item * 64 : 256 + (item + 1) * 64, lanes]
            for item in range(4)
        ]
        tendency = 1.0 - ocean_share * land[span]
        for item, variable in enumerate((3, 1, 2)):
            gain = gains[0, 0] if variable == 3 else gains[0, 1]
            updated[0, variable, span] = updated[0, variable, span] + tendency * gain * (
                sums[item] - sums[3] * fields[0, variable, span]
            )
    level_store(0).start()
    for level in range(levels):
        level_store(level).wait()


def shards(
    model_state,
    sea_mask,
    wave_speed,
    diffusivity,
    surface_gains,
    area_table,
    own_cells,
    target_cells,
    weight_ids,
    pair_counts,
    fold_map,
):
    levels = model_state.shape[2]
    windows = lax.axis_size("comp") - 1
    count_x = lax.axis_size("tx")
    packets = windows * NEAR
    anywhere = pl.BlockSpec(memory_space=pl.ANY)
    scalars = pl.BlockSpec(memory_space=pltpu.SMEM)
    f32, i32 = jnp.float32, jnp.int32
    dma = pltpu.SemaphoreType.DMA
    cells, values, rows, columns, folded = pl.pallas_call(
        exchange_kernel,
        out_shape=(
            jax.ShapeDtypeStruct((packets, 2 * GROUP, COLS), i32),
            jax.ShapeDtypeStruct((packets, 3 * GROUP, COLS), f32),
            jax.ShapeDtypeStruct((2, 40, COLS), f32),
            jax.ShapeDtypeStruct((2, ROWS, 128), f32),
            jax.ShapeDtypeStruct((count_x, ROWS, 128), f32),
        ),
        in_specs=[scalars] + [anywhere] * 5,
        out_specs=[anywhere] * 5,
        scratch_shapes=[
            pltpu.VMEM((4, levels, ROWS, COLS), f32),
            pltpu.VMEM((ROWS, COLS), i32),
            pltpu.VMEM((NEAR, GROUP * COLS), i32),
            pltpu.VMEM((NEAR, GROUP * COLS), i32),
            pltpu.VMEM((NEAR, GROUP * COLS), i32),
            pltpu.VMEM((3 * COLS, 2 * ROWS), jnp.bfloat16),
            pltpu.VMEM((NEAR, 2 * GROUP, COLS), i32),
            pltpu.VMEM((NEAR, 3 * GROUP, COLS), f32),
            pltpu.VMEM((2, 40, COLS), f32),
            pltpu.VMEM((2, ROWS, 128), f32),
            dma((6,)),
            dma((packets,)),
            dma((packets,)),
            dma((packets,)),
            dma((packets,)),
            dma((4,)),
            dma((4,)),
            dma((count_x,)),
            dma((count_x,)),
        ],
        compiler_params=pltpu.CompilerParams(
            collective_id=0, has_side_effects=True, vmem_limit_bytes=32 * 2**20
        ),
        name="exchange",
    )(pair_counts, model_state, sea_mask, own_cells, target_cells, weight_ids)
    return pl.pallas_call(
        step_kernel,
        out_shape=jax.ShapeDtypeStruct(model_state.shape, f32),
        in_specs=[scalars] * 3 + [anywhere] * 9,
        out_specs=anywhere,
        scratch_shapes=[
            pltpu.VMEM((levels, 4, ROWS, COLS), f32),
            pltpu.VMEM((levels, 4, ROWS, COLS), f32),
            pltpu.VMEM((ROWS, COLS), f32),
            pltpu.VMEM(area_table.shape, f32),
            pltpu.VMEM((ROWS,), i32),
            pltpu.VMEM(cells.shape, i32),
            pltpu.VMEM(values.shape, f32),
            pltpu.VMEM(rows.shape, f32),
            pltpu.VMEM(columns.shape, f32),
            pltpu.VMEM(folded.shape, f32),
            pltpu.VMEM((ROWS, COLS), i32),
            pltpu.VMEM((packets, GROUP, COLS), i32),
            pltpu.VMEM((packets, GROUP, COLS), i32),
            pltpu.VMEM((packets, 8, GROUP, COLS), f32),
            pltpu.VMEM((2 * 4 * 64, 4 * COLS), jnp.bfloat16),
            pltpu.VMEM((2 * COLS, 4 * COLS), jnp.bfloat16),
            pltpu.VMEM((2 * 4 * 64, 2 * COLS), f32),
            dma((8,)),
            dma((levels,)),
            dma((levels,)),
        ],
        compiler_params=pltpu.CompilerParams(vmem_limit_bytes=48 * 2**20),
        name="step",
    )(
        wave_speed,
        diffusivity,
        surface_gains,
        model_state,
        sea_mask,
        area_table,
        fold_map,
        cells,
        values,
        rows,
        columns,
        folded,
    )


def solution(mesh):
    in_specs = (
        P("comp", None, None, "tx", "ty"),
        P("comp", "tx", "ty"),
        P("comp", None),
        P("comp", None),
        P("comp", None),
        P(),
        P("comp", ("tx", "ty"), None, None),
        P("comp", ("tx", "ty"), None, None),
        P("comp", ("tx", "ty"), None, None),
        P("comp", ("tx", "ty"), None),
        P(),
    )
    out_specs = P("comp", None, None, "tx", "ty")
    return jax.shard_map(shards, mesh=mesh, in_specs=in_specs, out_specs=out_specs, check_vma=False)
```

time: 823 us -> 52.9 us (0.06); the launches traced: 810 us -> 52.2 us
  local copies, waits for them, and re-layouts: 335 us -> 6.05 us
  other arithmetic: 285 us -> 0 us
  matrix products: 149 us -> 0 us
  Pallas kernels: 0 us -> 46.1 us
  starting transfers between devices: 21 us -> 0 us
  blocking collectives: 17.7 us -> 0 us
    concatenate x2 -> x0, other arithmetic: 232 us -> none  [with_halo(): array = jnp.concatenate([before, array, after], axis=dim)]
    dot_general x6 -> x0, matrix products: 149 us -> none  [the longest x1 87.6 us: pick_cells(): jnp.einsum('kvc,kc->vk', chosen_rows, col_table, precision=lax.Precision....]
    squeeze x11 -> x0, local copies, waits for them, and re-layouts: 133 us -> none  [the longest x2 64.8 us: shards(): pressure_pad, tracer_pad = (scalars[0], scalars[1])]
    slice x14 -> x0, local copies, waits for them, and re-layouts: 76.3 us -> none  [the longest x1 34.6 us: shards(): pressure_pad, tracer_pad = (scalars[0], scalars[1])]
    gather x4 -> x0, local copies, waits for them, and re-layouts: 52.7 us -> none  [the longest x2 51.2 us: shards(): weight = jnp.where(living, area_table[weight_ids[0, 0]], 0.0)]
    another operation x3 -> x0, local copies, waits for them, and re-layouts: 52 us -> none  [the longest x1 26 us: shards(): jnp.stack([new_zonal, new_meridional])]
    pallas_call x0 -> x2, Pallas kernels: none -> 46.1 us  [the longest x1 23.4 us: shards(): pl.pallas_call(step_kernel, out_shape=jax.ShapeDtypeStruct(model_state.sh...]
    another operation x15 -> x0, other arithmetic: 23.7 us -> none  [the longest x1 8.47 us: shards(): jnp.stack([new_pressure, new_zonal, new_meridional, new_tracer])[None]]
  transfers between devices with their start and end apart: 12 -> 0, of which waited for: 0 -> 0; matrix products, arithmetic and copies ran while one was open for 87% -> 0% of each run, Pallas kernels for 0% -> 0%
where the time goes in v1:
time: 52.9 us; the launch traced here: 52.2 us
  Pallas kernels  46.1 us (87%)
  local copies, waits for them, and re-layouts  6.05 us (11%)
    pallas_call x1, Pallas kernels, shards(): pl.pallas_call(step_kernel, out_shape=jax.ShapeDtypeStruct(model_state.sh...  23.4 us
    pallas_call x1, Pallas kernels, shards(): pl.pallas_call(exchange_kernel, out_shape=(jax.ShapeDtypeStruct((packets,...  22.7 us
    unnamed x26, local copies, waits for them, and re-layouts  6.05 us

profile of v1, /device:TPU:6, one launch (start us, length us, event | category | flops | bytes accessed | tf_op | source)
XLA Modules:
  0.0 52.2 jit_solution(5149816138836494315)
XLA Ops:
  0.0 0.0 copy-start
  0.0 2.2 %copy-done = f32[1,4,8,128,256]{4,3,2,1,0:T(8,128)S(1)} copy-done((f32[1,4,8,128,256]{4,3,2,1,0:T(8,128)S(1)}, f32[1,4,8,128,256]{4,3,2,1,0:T(8,128)}, u32[]{:S(2)}) %copy-start) | copy-done | bytes 4194328
  2.2 0.0 copy-start.2
  2.2 0.9 %copy-done.2 = s32[1,128,256]{2,1,0:T(8,128)S(1)} copy-done((s32[1,128,256]{2,1,0:T(8,128)S(1)}, s32[1,128,256]{2,1,0:T(8,128)}, u32[]{:S(2)}) %copy-start.2) | copy-done | bytes 131096
  3.1 0.0 copy-start.4
  3.1 0.8 %copy-done.4 = s32[1,1,4,2048]{3,2,1,0:T(4,128)S(1)} copy-done((s32[1,1,4,2048]{3,2,1,0:T(4,128)S(1)}, s32[1,1,4,2048]{3,2,1,0:T(4,128)}, u32[]{:S(2)}) %copy-start.4) | copy-done | bytes 32792
  3.9 0.0 copy-start.5
  3.9 0.8 %copy-done.5 = s32[1,1,4,2048]{3,2,1,0:T(4,128)S(1)} copy-done((s32[1,1,4,2048]{3,2,1,0:T(4,128)S(1)}, s32[1,1,4,2048]{3,2,1,0:T(4,128)}, u32[]{:S(2)}) %copy-start.5) | copy-done | bytes 32792
  4.6 0.0 copy-start.6
  4.6 0.8 %copy-done.6 = s32[1,1,4,2048]{3,2,1,0:T(4,128)S(1)} copy-done((s32[1,1,4,2048]{3,2,1,0:T(4,128)S(1)}, s32[1,1,4,2048]{3,2,1,0:T(4,128)}, u32[]{:S(2)}) %copy-start.6) | copy-done | bytes 32792
  5.4 0.0 copy-start.9
  5.4 0.7 %copy-done.9 = s32[1,1,4]{2,1,0:T(1,128)S(1)} copy-done((s32[1,1,4]{2,1,0:T(1,128)S(1)}, s32[1,1,4]{2,1,0:T(1,128)}, u32[]{:S(2)}) %copy-start.9) | copy-done | bytes 40
  6.0 0.0 copy-start.1
  6.0 0.0 copy-start.3
  6.0 0.0 copy-start.7
  6.0 0.0 copy-start.8
  6.0 0.0 copy-start.10
  6.0 0.0 copy-start.11
  6.1 0.0 copy-start.12
  6.1 22.7 %exchange.1 = (s32[12,16,256]{2,1,0:T(8,128)S(1)}, f32[12,24,256]{2,1,0:T(8,128)S(1)}, f32[2,40,256]{2,1,0:T(8,128)S(1)}, f32[2,128,128]{2,1,0:T(8,128)S(1)}, f32[4,128,128]{2,1,0:T(8,128)S(1)}) custom-call(s32[1,1,4]{2,1,0:T(1,128)S(1)} %copy-done.9, f32[1,4,8,128,256]{4,3,2,1,0:T(8,128)S(1)} %copy-done, s32[1,128,256]{2,1,0:T(8,128)S(1)} %copy-done.2, ...), custom_call_target="tpu_custom_call" | custom-call | tf_op jit(solution)/shard_map/exchange/pallas_call | solution.py:638
  28.8 0.0 copy-done.1
  28.8 0.0 copy-done.3
  28.8 0.0 copy-done.7
  28.8 0.0 copy-done.8
  28.8 0.0 copy-done.10
  28.8 0.0 copy-done.11
  28.9 0.0 copy-done.12
  28.9 23.4 %step.1 = f32[1,4,8,128,256]{4,3,2,1,0:T(8,128)} custom-call(f32[1,8]{1,0:T(1,128)S(1)} %copy-done.10, f32[1,8]{1,0:T(1,128)S(1)} %copy-done.11, f32[1,3]{1,0:T(1,128)S(1)} %copy-done.12, f32[1,4,8,128,256]{4,3,2,1,0:T(8,128)S(1)} %copy-done.1, s32[1,128,256]{2,1,0:T(8,128)S(1)} %copy-done.3, f32[256]{0:T(256)S(1)} %copy-done.8, s32[512]{0:T(512)S(1)} %copy-done.7, ...), custom_call_target="tpu_custom_call" | custom-call | tf_op jit(solution)/shard_map/step/pallas_call | solution.py:675
Async XLA Ops:
  0.0 2.2 %copy-start = (f32[1,4,8,128,256]{4,3,2,1,0:T(8,128)S(1)}, f32[1,4,8,128,256]{4,3,2,1,0:T(8,128)}, u32[]{:S(2)}) copy-start(f32[1,4,8,128,256]{4,3,2,1,0:T(8,128)} %state.3) | copy-start | bytes 12582916
  2.2 0.9 %copy-start.2 = (s32[1,128,256]{2,1,0:T(8,128)S(1)}, s32[1,128,256]{2,1,0:T(8,128)}, u32[]{:S(2)}) copy-start(s32[1,128,256]{2,1,0:T(8,128)} %mask.3) | copy-start | bytes 393220
  3.1 0.8 %copy-start.4 = (s32[1,1,4,2048]{3,2,1,0:T(4,128)S(1)}, s32[1,1,4,2048]{3,2,1,0:T(4,128)}, u32[]{:S(2)}) copy-start(s32[1,1,4,2048]{3,2,1,0:T(4,128)} %own.1) | copy-start | bytes 98308
  3.9 0.8 %copy-start.5 = (s32[1,1,4,2048]{3,2,1,0:T(4,128)S(1)}, s32[1,1,4,2048]{3,2,1,0:T(4,128)}, u32[]{:S(2)}) copy-start(s32[1,1,4,2048]{3,2,1,0:T(4,128)} %target.1) | copy-start | bytes 98308
  4.6 0.8 %copy-start.6 = (s32[1,1,4,2048]{3,2,1,0:T(4,128)S(1)}, s32[1,1,4,2048]{3,2,1,0:T(4,128)}, u32[]{:S(2)}) copy-start(s32[1,1,4,2048]{3,2,1,0:T(4,128)} %ids.1) | copy-start | bytes 98308
  5.4 0.7 %copy-start.9 = (s32[1,1,4]{2,1,0:T(1,128)S(1)}, s32[1,1,4]{2,1,0:T(1,128)}, u32[]{:S(2)}) copy-start(s32[1,1,4]{2,1,0:T(1,128)} %counts.1) | copy-start | bytes 52
  6.0 22.8 %copy-start.1 = (f32[1,4,8,128,256]{4,3,2,1,0:T(8,128)S(1)}, f32[1,4,8,128,256]{4,3,2,1,0:T(8,128)}, u32[]{:S(2)}) copy-start(f32[1,4,8,128,256]{4,3,2,1,0:T(8,128)} %state.3) | copy-start | bytes 12582916
  6.0 22.8 %copy-start.3 = (s32[1,128,256]{2,1,0:T(8,128)S(1)}, s32[1,128,256]{2,1,0:T(8,128)}, u32[]{:S(2)}) copy-start(s32[1,128,256]{2,1,0:T(8,128)} %mask.3) | copy-start | bytes 393220
  6.0 22.8 %copy-start.7 = (s32[512]{0:T(512)S(1)}, s32[512]{0:T(512)}, u32[]{:S(2)}) copy-start(s32[512]{0:T(512)} %fold_map.1) | copy-start | bytes 6148
  6.0 22.8 %copy-start.8 = (f32[256]{0:T(256)S(1)}, f32[256]{0:T(256)}, u32[]{:S(2)}) copy-start(f32[256]{0:T(256)} %area.1) | copy-start | bytes 3076
  6.0 22.8 %copy-start.10 = (f32[1,8]{1,0:T(1,128)S(1)}, f32[1,8]{1,0:T(1,128)}, u32[]{:S(2)}) copy-start(f32[1,8]{1,0:T(1,128)} %wave.1) | copy-start | bytes 100
  6.0 22.8 %copy-start.11 = (f32[1,8]{1,0:T(1,128)S(1)}, f32[1,8]{1,0:T(1,128)}, u32[]{:S(2)}) copy-start(f32[1,8]{1,0:T(1,128)} %spread.1) | copy-start | bytes 100
  6.1 22.8 %copy-start.12 = (f32[1,3]{1,0:T(1,128)S(1)}, f32[1,3]{1,0:T(1,128)}, u32[]{:S(2)}) copy-start(f32[1,3]{1,0:T(1,128)} %gains.1) | copy-start | bytes 40

commit v2 on v1

v2 whole, which is shorter than its diff:
```python
import jax
import jax.numpy as jnp
from jax import lax
from jax.experimental import pallas as pl
from jax.experimental.pallas import tpu as pltpu
from jax.sharding import PartitionSpec as P

MESH = pl.DeviceIdType.MESH
NEAR = 4
ROWS = 128
COLS = 256
f32 = jnp.float32
i32 = jnp.int32
f8 = jnp.float8_e4m3fn
dma = pltpu.SemaphoreType.DMA
GROUP = 8
BATCH = 8


def exchange_kernel(
    counts,
    state,
    mask,
    own,
    target,
    ids,
    area,
    fold_map,
    places_out,
    weights_out,
    live_out,
    values_out,
    rows_out,
    columns_out,
    fields,
    sea,
    own_v,
    target_v,
    ids_v,
    area_v,
    fold_v,
    surface,
    early,
    late,
    rows_in,
    columns_in,
    arrived,
    places,
    weights,
    live,
    rows_got,
    columns_got,
    fold_got,
    load_sem,
    store_sem,
    early_send,
    early_recv,
    late_send,
    late_recv,
    edge_send,
    edge_recv,
    fold_send,
    fold_recv,
):
    levels = fields.shape[1]
    comps = lax.axis_size("comp")
    windows = comps - 1
    count_x = lax.axis_size("tx")
    count_y = lax.axis_size("ty")
    positions = count_x * count_y
    comp = lax.axis_index("comp")
    ix = lax.axis_index("tx")
    iy = lax.axis_index("ty")
    place = ix * count_y + iy
    is_ocean = comp == windows
    is_window = comp != windows
    on_fold = jnp.logical_and(is_ocean, iy == count_y - 1)
    offsets = [n % 2 + (n // 2) * count_y for n in range(NEAR)]

    def device_at(component, position):
        return (component, lax.div(position, count_y), lax.rem(position, count_y))

    loads = [
        pltpu.make_async_copy(target.at[0, 0], target_v, load_sem.at[0]),
        pltpu.make_async_copy(ids.at[0, 0], ids_v, load_sem.at[1]),
        pltpu.make_async_copy(own.at[0, 0], own_v, load_sem.at[2]),
        pltpu.make_async_copy(state.at[0, :, 0], fields.at[:, 0], load_sem.at[3]),
        pltpu.make_async_copy(
            state.at[0, :, pl.ds(1, levels - 1)], fields.at[:, pl.ds(1, levels - 1)], load_sem.at[4]
        ),
        pltpu.make_async_copy(mask.at[0], sea, load_sem.at[5]),
        pltpu.make_async_copy(area, area_v, load_sem.at[6]),
        pltpu.make_async_copy(fold_map.at[pl.ds(ix * ROWS, ROWS)], fold_v, load_sem.at[7]),
    ]
    for load in loads:
        load.start()

    west = (comp, lax.rem(ix + count_x - 1, count_x), iy)
    east = (comp, lax.rem(ix + 1, count_x), iy)
    south = (comp, ix, lax.rem(iy + count_y - 1, count_y))
    north = (comp, ix, lax.rem(iy + 1, count_y))

    barrier = pltpu.get_barrier_semaphore()
    for neighbour in (west, east, south, north):
        pl.semaphore_signal(barrier, inc=1, device_id=neighbour, device_id_type=MESH)
    sources = [lax.rem(place + positions - offset, positions) for offset in offsets]

    @pl.when(is_ocean)
    def _():
        for source in sources:
            for window in range(windows):
                pl.semaphore_signal(
                    barrier, inc=1, device_id=device_at(window, source), device_id_type=MESH
                )

    @pl.when(is_window)
    def _():
        for source in sources:
            pl.semaphore_signal(
                barrier, inc=1, device_id=device_at(windows, source), device_id_type=MESH
            )

    @pl.when(on_fold)
    def _():
        for step in range(1, count_x):
            pl.semaphore_signal(
                barrier,
                inc=1,
                device_id=(comp, lax.rem(ix + step, count_x), iy),
                device_id_type=MESH,
            )

    loads[0].wait()
    loads[1].wait()
    lane = lax.broadcasted_iota(jnp.int32, (1, COLS), 1)
    for n in range(NEAR):
        limit = counts[0, 0, n]
        for row in range(GROUP):
            span = slice(row * COLS, (row + 1) * COLS)
            cell = target_v[n : n + 1, span]
            early[n, row : row + 1] = jnp.where(lane + row * COLS < limit, cell, -1)
            early[n, GROUP + row : GROUP + row + 1] = ids_v[n : n + 1, span]

    slot = jnp.where(is_ocean, 0, comp * NEAR)

    def packet_copy(kind, n, window, component):
        position = lax.rem(place + offsets[n], positions)
        source, target_ref, send, recv = {
            "early": (early, arrived, early_send, early_recv),
            "late": (late, values_out, late_send, late_recv),
        }[kind]
        return pltpu.make_async_remote_copy(
            src_ref=source.at[n],
            dst_ref=target_ref.at[slot + n],
            send_sem=send.at[n * windows + window],
            recv_sem=recv.at[slot + n],
            device_id=device_at(component, position),
            device_id_type=MESH,
        )

    def send_packets(kind, n):
        @pl.when(is_ocean)
        def _():
            for window in range(windows):
                packet_copy(kind, n, window, window).start()

        @pl.when(is_window)
        def _():
            packet_copy(kind, n, 0, windows).start()

    @pl.when(is_window)
    def _():
        pl.semaphore_wait(barrier, 4 + NEAR)

    @pl.when(jnp.logical_and(is_ocean, iy != count_y - 1))
    def _():
        pl.semaphore_wait(barrier, 4 + windows * NEAR)

    @pl.when(on_fold)
    def _():
        pl.semaphore_wait(barrier, 4 + windows * NEAR + count_x - 1)

    for n in range(NEAR):
        send_packets("early", n)

    loads[2].wait()
    loads[3].wait()
    for at, variable in enumerate((3, 1, 2)):
        turned = jnp.transpose(fields[variable, 0])
        high = turned.astype(jnp.bfloat16)
        low = (turned - high.astype(jnp.float32)).astype(jnp.bfloat16)
        surface[at * COLS : (at + 1) * COLS, 0:ROWS] = high
        surface[at * COLS : (at + 1) * COLS, ROWS : 2 * ROWS] = low

    row_ids = lax.broadcasted_iota(jnp.int32, (ROWS, COLS), 0)
    col_ids = lax.broadcasted_iota(jnp.int32, (COLS, COLS), 0)

    def pick(n):
        def pick_row(row, carry):
            cell = own_v[n : n + 1, pl.ds(pl.multiple_of(row * COLS, COLS), COLS)]
            hot = jnp.where(row_ids == (cell >> 8), 1.0, 0.0).astype(jnp.bfloat16)
            chosen = jnp.dot(
                surface[...],
                jnp.concatenate([hot, hot], axis=0),
                preferred_element_type=jnp.float32,
            )
            here = col_ids == (cell & (COLS - 1))
            for at in range(3):
                part = jnp.where(here, chosen[at * COLS : (at + 1) * COLS], 0.0)
                late[n, pl.ds(at * GROUP + row, 1), :] = jnp.sum(part, axis=0, keepdims=True)
            return carry

        lax.fori_loop(0, GROUP, pick_row, 0, unroll=8)

    edge_copies = []
    for at, device in enumerate((west, east)):
        edge_copies.append(
            pltpu.make_async_remote_copy(
                src_ref=rows_in.at[at],
                dst_ref=rows_got.at[1 - at],
                send_sem=edge_send.at[at],
                recv_sem=edge_recv.at[1 - at],
                device_id=device,
                device_id_type=MESH,
            )
        )
    for at, device in enumerate((south, north)):
        edge_copies.append(
            pltpu.make_async_remote_copy(
                src_ref=columns_in.at[at],
                dst_ref=columns_got.at[1 - at],
                send_sem=edge_send.at[2 + at],
                recv_sem=edge_recv.at[2 + 1 - at],
                device_id=device,
                device_id_type=MESH,
            )
        )

    def fold_copy(step):
        return pltpu.make_async_remote_copy(
            src_ref=columns_in.at[1],
            dst_ref=fold_got.at[ix],
            send_sem=fold_send.at[step],
            recv_sem=fold_recv.at[step],
            device_id=(comp, lax.rem(ix + step, count_x), iy),
            device_id_type=MESH,
        )

    fold_keep = pltpu.make_async_copy(columns_in.at[1], fold_got.at[ix], fold_send.at[0])

    def send_edges():
        loads[4].wait()
        loads[5].wait()
        for at, (near, far) in enumerate(((0, 1), (ROWS - 1, ROWS - 2))):
            for level in range(levels):
                for item, (variable, row) in enumerate(((0, near), (0, far), (1, near), (3, near))):
                    rows_in[at, item * 8 + level : item * 8 + level + 1] = fields[
                        variable, level, row : row + 1, :
                    ]
            rows_in[at, 32:33] = sea[near : near + 1].astype(jnp.float32)
        lanes = lax.broadcasted_iota(jnp.int32, (ROWS, 128), 1)
        for at, (near, far) in enumerate(((0, 1), (127, 126))):
            half = slice(at * 128, (at + 1) * 128)
            columns_in[at] = jnp.where(
                lanes == 32,
                pltpu.roll(sea[:, half].astype(jnp.float32), (32 - near) % 128, 1),
                0.0,
            )

            def add_level(level, carry):
                packed = columns_in[at]
                for item, (variable, column) in enumerate(
                    ((0, near), (0, far), (2, near), (3, near))
                ):
                    place_at = item * 8 + level
                    turned = pltpu.roll(
                        fields[variable, level, :, half],
                        lax.rem(place_at + (128 - column), 128),
                        1,
                    )
                    packed = jnp.where(lanes == place_at, turned, packed)
                columns_in[at] = packed
                return carry

            lax.fori_loop(0, levels, add_level, 0, unroll=2)
        for copy in edge_copies:
            copy.start()

        @pl.when(on_fold)
        def _():
            fold_keep.start()
            for step in range(1, count_x):
                fold_copy(step).start()

    pick(0)
    send_packets("late", 0)
    for n in range(1, NEAR):
        pick(n)
        send_packets("late", n)
    send_edges()

    def wait_slot(kind, at):
        target_ref, recv, source = {
            "early": (arrived, early_recv, early),
            "late": (values_out, late_recv, late),
        }[kind]
        pltpu.make_async_remote_copy(
            src_ref=source.at[0],
            dst_ref=target_ref.at[at],
            send_sem=early_send.at[0],
            recv_sem=recv.at[at],
            device_id=west,
            device_id_type=MESH,
        ).wait_recv()

    def finish(kind):
        @pl.when(is_ocean)
        def _():
            for n in range(NEAR):
                for window in range(windows):
                    packet_copy(kind, n, window, window).wait_send()
            for at in range(windows * NEAR):
                wait_slot(kind, at)

        @pl.when(is_window)
        def _():
            for n in range(NEAR):
                packet_copy(kind, n, 0, windows).wait_send()
            for at in range(NEAR):
                wait_slot(kind, at)

    loads[6].wait()
    loads[7].wait()
    spare = windows * NEAR * GROUP
    places[0, spare : spare + GROUP] = jnp.zeros((GROUP, COLS), i32)
    places[1, spare : spare + GROUP] = jnp.full((GROUP, COLS), -1, i32)
    table = [
        jnp.broadcast_to(area_v[at * 128 : (at + 1) * 128][None], (GROUP, 128)) for at in range(2)
    ]
    slot_ids = lax.broadcasted_iota(
        jnp.int32, (GROUP, COLS), 0
    ) * COLS + lax.broadcasted_iota(jnp.int32, (GROUP, COLS), 1)
    mine = jnp.logical_or(slot_ids - 3 * ((slot_ids * 43691) >> 17) == comp, is_ocean)
    finish("early")

    def place_packets(group, carry):
        for n in range(NEAR):
            at = group * NEAR + n
            cell = arrived[at, 0:GROUP]
            entry = arrived[at, GROUP : 2 * GROUP]
            lines = pl.ds(pl.multiple_of(at * GROUP, GROUP), GROUP)
            for half in range(2):
                span = slice(half * 128, (half + 1) * 128)
                index = entry[:, span]
                low = jnp.take_along_axis(table[0], index & 127, axis=1, mode="promise_in_bounds")
                high = jnp.take_along_axis(table[1], index & 127, axis=1, mode="promise_in_bounds")
                weights[lines, span] = jnp.where(index < 128, low, high)
            row = cell >> 8
            places[0, lines] = row & 63
            alive = jnp.logical_and(cell >= 0, mine)
            places[1, lines] = jnp.where(alive, ((row >> 6) << 8) + (cell & (COLS - 1)), -1)
            used = jnp.sum(jnp.where(cell >= 0, 1.0, 0.0), axis=0, keepdims=True)
            used = jnp.sum(used, axis=1, keepdims=True)
            live[pl.ds(at, 1)] = jnp.broadcast_to(used, (1, 128)).astype(jnp.int32)
        return carry

    lax.fori_loop(0, jnp.where(is_ocean, windows, 1), place_packets, 0)
    stores = [
        pltpu.make_async_copy(places, places_out, store_sem.at[0]),
        pltpu.make_async_copy(weights, weights_out, store_sem.at[1]),
        pltpu.make_async_copy(live, live_out, store_sem.at[2]),
        pltpu.make_async_copy(rows_got, rows_out, store_sem.at[3]),
        pltpu.make_async_copy(columns_got, columns_out, store_sem.at[4]),
    ]
    for store in stores[:3]:
        store.start()

    for copy in edge_copies:
        copy.wait_send()
        copy.wait_recv()
    one = jnp.float32(1.0)
    zero = jnp.float32(0.0)
    rows_got[0] = rows_got[0] * jnp.where(jnp.logical_or(is_ocean, ix > 0), one, zero)
    rows_got[1] = rows_got[1] * jnp.where(jnp.logical_or(is_ocean, ix < count_x - 1), one, zero)
    columns_got[0] = columns_got[0] * jnp.where(iy > 0, one, zero)
    columns_got[1] = columns_got[1] * jnp.where(iy < count_y - 1, one, zero)

    @pl.when(on_fold)
    def _():
        fold_keep.wait()
        for step in range(1, count_x):
            fold_copy(step).wait_send()
            fold_copy(step).wait_recv()
        wanted = jnp.transpose(jnp.broadcast_to(fold_v[...][None], (ROWS, ROWS)))
        lanes = lax.broadcasted_iota(jnp.int32, (ROWS, 128), 1)
        gathered = jnp.zeros((ROWS, 128), f32)
        for block in range(count_x):
            hot = jnp.where(wanted == lanes + block * ROWS, 1.0, 0.0).astype(jnp.bfloat16)
            rest = fold_got[block]
            for part in range(3):
                piece = rest.astype(jnp.bfloat16)
                rest = rest - piece.astype(f32)
                gathered += jnp.dot(hot, piece, preferred_element_type=f32)
        turned = jnp.logical_and(lanes >= 16, lanes < 24)
        columns_got[1] = jnp.where(turned, -gathered, gathered)

    for store in stores[3:]:
        store.start()
    finish("late")
    for store in stores:
        store.wait()


def step_kernel(
    wave,
    spread,
    gains,
    state,
    mask,
    places,
    weights,
    live,
    values,
    rows,
    columns,
    result,
    fields,
    updated,
    land,
    places_v,
    weights_v,
    values_v,
    rows_v,
    columns_v,
    sea_v,
    addends,
    live_s,
    order,
    left,
    right,
    total,
    load_sem,
    level_sem,
    store_sem,
):
    levels = fields.shape[0]
    windows = lax.axis_size("comp") - 1
    count_x = lax.axis_size("tx")
    count_y = lax.axis_size("ty")
    comp = lax.axis_index("comp")
    ix = lax.axis_index("tx")
    iy = lax.axis_index("ty")
    is_ocean = comp == windows
    packets = values_v.shape[0]

    def level_load(level):
        return pltpu.make_async_copy(state.at[0, :, level], fields.at[level], level_sem.at[level])

    def level_store(level):
        return pltpu.make_async_copy(
            updated.at[level], result.at[0, :, level], store_sem.at[level]
        )

    loads = [
        pltpu.make_async_copy(live, live_s, load_sem.at[0]),
        pltpu.make_async_copy(values, values_v, load_sem.at[1]),
        pltpu.make_async_copy(weights, weights_v, load_sem.at[2]),
        pltpu.make_async_copy(places, places_v, load_sem.at[3]),
        pltpu.make_async_copy(mask.at[0], sea_v, load_sem.at[4]),
        pltpu.make_async_copy(rows, rows_v, load_sem.at[5]),
        pltpu.make_async_copy(columns, columns_v, load_sem.at[6]),
    ]
    for load in loads:
        load.start()
    for level in range(levels):
        level_load(level).start()

    spare = packets * GROUP
    addends[:, spare : spare + GROUP] = jnp.zeros((12, GROUP, COLS), f32)
    total[...] = jnp.zeros_like(total)
    for at in range(spare + GROUP):
        order[at] = spare
    loads[0].wait()

    def list_packet(at, count):
        lines = (live_s[at, 0] + COLS - 1) // COLS

        def list_row(row, carry):
            order[count + row] = at * GROUP + row
            return carry

        lax.fori_loop(0, lines, list_row, 0)
        return count + lines

    live_lines = lax.fori_loop(0, jnp.where(is_ocean, packets, NEAR), list_packet, 0)

    for load in loads[1:]:
        load.wait()

    def split_packets(group, carry):
        for n in range(NEAR):
            at = group * NEAR + n
            lines = pl.ds(pl.multiple_of(at * GROUP, GROUP), GROUP)
            weight = weights_v[lines] * 64.0
            for item in range(4):
                value = weight
                if item < 3:
                    value = weight * values_v[at, item * GROUP : (item + 1) * GROUP]
                for part in range(3):
                    piece = value.astype(f8).astype(f32)
                    addends[part * 4 + item, lines] = piece
                    value = (value - piece) * 16.0
        return carry

    lax.fori_loop(0, jnp.where(is_ocean, packets // NEAR, 1), split_packets, 0)
    land[...] = 1.0 - sea_v[...].astype(jnp.float32)
    one = jnp.float32(1.0)
    zero = jnp.float32(0.0)
    valid_west = jnp.where(jnp.logical_or(is_ocean, ix > 0), one, zero)
    valid_east = jnp.where(jnp.logical_or(is_ocean, ix < count_x - 1), one, zero)
    valid_south = jnp.where(iy > 0, one, zero)
    valid_north = jnp.where(jnp.logical_or(is_ocean, iy < count_y - 1), one, zero)

    row_ids = lax.broadcasted_iota(jnp.int32, (ROWS, COLS), 0)
    col_ids = lax.broadcasted_iota(jnp.int32, (ROWS, COLS), 1)
    is_first_row = row_ids == 0
    is_last_row = row_ids == ROWS - 1
    is_first_col = col_ids == 0
    is_last_col = col_ids == COLS - 1
    ocean_share = jnp.where(is_ocean, one, zero)

    def before_x(field, edge):
        return jnp.where(is_first_row, edge, pltpu.roll(field, 1, 0))

    def after_x(field, edge):
        return jnp.where(is_last_row, edge, pltpu.roll(field, ROWS - 1, 0))

    def before_y(field, edge):
        return jnp.where(is_first_col, edge, pltpu.roll(field, 1, 1))

    def after_y(field, edge):
        return jnp.where(is_last_col, edge, pltpu.roll(field, COLS - 1, 1))

    def stencil(level):
        level_load(level).wait()
        pressure = fields[level, 0]
        zonal = fields[level, 1]
        meridional = fields[level, 2]
        tracer = fields[level, 3]
        half_wave = 0.5 * wave[0, level]
        drag = jnp.where(is_ocean, one, jnp.where(level == 0, gains[0, 2], zero))
        keeping = 1.0 - drag * land[...]
        tendency = 1.0 - ocean_share * land[...]
        edge_rows = [
            [rows_v[side, pl.ds(item * 8 + level, 1), :] for item in range(4)] for side in range(2)
        ]
        turn = lax.rem(128 - level, 128)
        shifted = [pltpu.roll(columns_v[side], turn, 1) for side in range(2)]
        edge_cols = [
            [shifted[side][:, item * 8 : item * 8 + 1] for item in range(4)] for side in range(2)
        ]
        row_keep = [
            (1.0 - drag * (1.0 - rows_v[0, 32:33, :])) * valid_west,
            (1.0 - drag * (1.0 - rows_v[1, 32:33, :])) * valid_east,
        ]
        col_keep = [
            (1.0 - drag * (1.0 - columns_v[0, :, 32:33])) * valid_south,
            (1.0 - drag * (1.0 - columns_v[1, :, 32:33])) * valid_north,
        ]
        new_zonal = keeping * (
            zonal
            - half_wave
            * (after_x(pressure, edge_rows[1][0]) - before_x(pressure, edge_rows[0][0]))
        )
        new_meridional = keeping * (
            meridional
            - half_wave
            * (after_y(pressure, edge_cols[1][0]) - before_y(pressure, edge_cols[0][0]))
        )
        zonal_west = row_keep[0] * (
            edge_rows[0][2] - half_wave * (pressure[0:1] - edge_rows[0][1])
        )
        zonal_east = row_keep[1] * (
            edge_rows[1][2] - half_wave * (edge_rows[1][1] - pressure[ROWS - 1 : ROWS])
        )
        meridional_south = col_keep[0] * (
            edge_cols[0][2] - half_wave * (pressure[:, 0:1] - edge_cols[0][1])
        )
        meridional_north = col_keep[1] * (
            edge_cols[1][2] - half_wave * (edge_cols[1][1] - pressure[:, COLS - 1 : COLS])
        )
        divergence = (
            after_x(new_zonal, zonal_east)
            - before_x(new_zonal, zonal_west)
            + after_y(new_meridional, meridional_north)
            - before_y(new_meridional, meridional_south)
        )
        laplace = (
            after_x(tracer, edge_rows[1][3])
            + before_x(tracer, edge_rows[0][3])
            + after_y(tracer, edge_cols[1][3])
            + before_y(tracer, edge_cols[0][3])
            - 4.0 * tracer
        )
        updated[level, 0] = pressure - half_wave * divergence
        updated[level, 1] = new_zonal
        updated[level, 2] = new_meridional
        updated[level, 3] = tracer + spread[0, level] * tendency * laplace

    narrow_ids = lax.broadcasted_iota(jnp.int16, (64, COLS), 0)
    wide_ids = lax.broadcasted_iota(jnp.int16, (2 * COLS, COLS), 0)
    one16 = jnp.ones((), jnp.bfloat16)
    zero16 = jnp.zeros((), jnp.bfloat16)

    def repeated(line, count, kind):
        tile = jnp.broadcast_to(line, (16, COLS)).astype(kind)
        return jnp.concatenate([tile] * (count // 16), axis=0)

    def scatter(batch):
        for at in range(BATCH):
            line = pl.ds(order[batch * BATCH + at], 1)
            span = slice(at * COLS, (at + 1) * COLS)
            here = narrow_ids == repeated(places_v[0, line, :], 64, jnp.int16)
            for item in range(4):
                for part in range(3):
                    value = addends[part * 4 + item, line, :]
                    lead = (part * 4 + item) * 64
                    left[lead : lead + 64, span] = jnp.where(
                        here, repeated(value, 64, jnp.bfloat16), zero16
                    ).astype(f8)
            there = wide_ids == repeated(places_v[1, line, :], 2 * COLS, jnp.int16)
            right[:, span] = jnp.where(there, one16, zero16).astype(f8)
        total[...] += lax.dot_general(
            left[...],
            right[...],
            (((1,), (1,)), ((), ())),
            preferred_element_type=jnp.float32,
        )

    def level_step(level, carry):
        stencil(level)
        scatter(level)

        @pl.when(level > 0)
        def _():
            level_store(level).start()

        return carry

    lax.fori_loop(0, levels, level_step, 0)

    def extra_step(batch, carry):
        scatter(batch)
        return carry

    lax.fori_loop(levels, jnp.maximum(levels, (live_lines + BATCH - 1) // BATCH), extra_step, 0)

    for half in range(2):
        span = slice(half * 64, (half + 1) * 64)
        lanes = slice(half * COLS, (half + 1) * COLS)
        sums = [
            total[item * 64 : (item + 1) * 64, lanes] * (1.0 / 64.0)
            + total[256 + item * 64 : 256 + (item + 1) * 64, lanes] * (1.0 / 1024.0)
            + total[512 + item * 64 : 512 + (item + 1) * 64, lanes] * (1.0 / 16384.0)
            for item in range(4)
        ]
        tendency = 1.0 - ocean_share * land[span]
        for item, variable in enumerate((3, 1, 2)):
            gain = gains[0, 0] if variable == 3 else gains[0, 1]
            updated[0, variable, span] = updated[0, variable, span] + tendency * gain * (
                sums[item] - sums[3] * fields[0, variable, span]
            )
    level_store(0).start()
    for level in range(levels):
        level_store(level).wait()


def exchange_call(
    model_state, sea_mask, own_cells, target_cells, weight_ids, pair_counts, area_table, fold_map
):
    levels = model_state.shape[2]
    packets = (lax.axis_size("comp") - 1) * NEAR
    lines = packets * GROUP
    count_x = lax.axis_size("tx")
    anywhere = pl.BlockSpec(memory_space=pl.ANY)
    shapes = [
        ((2, lines + GROUP, COLS), i32),
        ((lines, COLS), f32),
        ((16, 128), i32),
        ((packets, 3 * GROUP, COLS), f32),
        ((2, 40, COLS), f32),
        ((2, ROWS, 128), f32),
    ]
    return pl.pallas_call(
        exchange_kernel,
        out_shape=tuple(jax.ShapeDtypeStruct(shape, kind) for shape, kind in shapes),
        in_specs=[pl.BlockSpec(memory_space=pltpu.SMEM)] + [anywhere] * 7,
        out_specs=[anywhere] * 6,
        scratch_shapes=[
            pltpu.VMEM((4, levels, ROWS, COLS), f32),
            pltpu.VMEM((ROWS, COLS), i32),
            pltpu.VMEM((NEAR, GROUP * COLS), i32),
            pltpu.VMEM((NEAR, GROUP * COLS), i32),
            pltpu.VMEM((NEAR, GROUP * COLS), i32),
            pltpu.VMEM(area_table.shape, f32),
            pltpu.VMEM((ROWS,), i32),
            pltpu.VMEM((3 * COLS, 2 * ROWS), jnp.bfloat16),
            pltpu.VMEM((NEAR, 2 * GROUP, COLS), i32),
            pltpu.VMEM((NEAR, 3 * GROUP, COLS), f32),
            pltpu.VMEM((2, 40, COLS), f32),
            pltpu.VMEM((2, ROWS, 128), f32),
            pltpu.VMEM((packets, 2 * GROUP, COLS), i32),
            pltpu.VMEM((2, lines + GROUP, COLS), i32),
            pltpu.VMEM((lines, COLS), f32),
            pltpu.VMEM((16, 128), i32),
            pltpu.VMEM((2, 40, COLS), f32),
            pltpu.VMEM((2, ROWS, 128), f32),
            pltpu.VMEM((count_x, ROWS, 128), f32),
            dma((8,)),
            dma((5,)),
            dma((packets,)),
            dma((packets,)),
            dma((packets,)),
            dma((packets,)),
            dma((4,)),
            dma((4,)),
            dma((count_x,)),
            dma((count_x,)),
        ],
        compiler_params=pltpu.CompilerParams(
            collective_id=0, has_side_effects=True, vmem_limit_bytes=60 * 2**20
        ),
        name="exchange",
    )(
        pair_counts,
        model_state,
        sea_mask,
        own_cells,
        target_cells,
        weight_ids,
        area_table,
        fold_map,
    )


def step_call(
    model_state,
    sea_mask,
    wave_speed,
    diffusivity,
    surface_gains,
    places,
    weights,
    live,
    values,
    rows,
    columns,
):
    levels = model_state.shape[2]
    lines = places.shape[1]
    anywhere = pl.BlockSpec(memory_space=pl.ANY)
    scalars = pl.BlockSpec(memory_space=pltpu.SMEM)
    return pl.pallas_call(
        step_kernel,
        out_shape=jax.ShapeDtypeStruct(model_state.shape, f32),
        in_specs=[scalars] * 3 + [anywhere] * 8,
        out_specs=anywhere,
        scratch_shapes=[
            pltpu.VMEM((levels, 4, ROWS, COLS), f32),
            pltpu.VMEM((levels, 4, ROWS, COLS), f32),
            pltpu.VMEM((ROWS, COLS), f32),
            pltpu.VMEM(places.shape, i32),
            pltpu.VMEM(weights.shape, f32),
            pltpu.VMEM(values.shape, f32),
            pltpu.VMEM(rows.shape, f32),
            pltpu.VMEM(columns.shape, f32),
            pltpu.VMEM((ROWS, COLS), i32),
            pltpu.VMEM((12, lines, COLS), f32),
            pltpu.SMEM(live.shape, i32),
            pltpu.SMEM((lines,), i32),
            pltpu.VMEM((3 * 4 * 64, BATCH * COLS), f8),
            pltpu.VMEM((2 * COLS, BATCH * COLS), f8),
            pltpu.VMEM((3 * 4 * 64, 2 * COLS), f32),
            dma((7,)),
            dma((levels,)),
            dma((levels,)),
        ],
        compiler_params=pltpu.CompilerParams(vmem_limit_bytes=60 * 2**20),
        name="step",
    )(
        wave_speed,
        diffusivity,
        surface_gains,
        model_state,
        sea_mask,
        places,
        weights,
        live,
        values,
        rows,
        columns,
    )


def shards(
    model_state,
    sea_mask,
    wave_speed,
    diffusivity,
    surface_gains,
    area_table,
    own_cells,
    target_cells,
    weight_ids,
    pair_counts,
    fold_map,
):
    exchanged = exchange_call(
        model_state,
        sea_mask,
        own_cells,
        target_cells,
        weight_ids,
        pair_counts,
        area_table,
        fold_map,
    )
    return step_call(
        model_state, sea_mask, wave_speed, diffusivity, surface_gains, *exchanged
    )


def solution(mesh):
    in_specs = (
        P("comp", None, None, "tx", "ty"),
        P("comp", "tx", "ty"),
        P("comp", None),
        P("comp", None),
        P("comp", None),
        P(),
        P("comp", ("tx", "ty"), None, None),
        P("comp", ("tx", "ty"), None, None),
        P("comp", ("tx", "ty"), None, None),
        P("comp", ("tx", "ty"), None),
        P(),
    )
    out_specs = P("comp", None, None, "tx", "ty")
    return jax.shard_map(shards, mesh=mesh, in_specs=in_specs, out_specs=out_specs, check_vma=False)
```

time: 52.9 us -> 35 us (0.66)
  Pallas kernels: 46.1 us -> 34.6 us
  local copies, waits for them, and re-layouts: 6.05 us -> 0 us
    pallas_call x2, Pallas kernels: 46.1 us -> 34.6 us  [the longest x1 20.8 us: exchange_call(): pl.pallas_call(exchange_kernel, out_shape=tuple((jax.ShapeDtypeStruct(sha...]
    unnamed x26 -> x0, local copies, waits for them, and re-layouts: 6.05 us -> none
where the time goes in v2:
time: 35 us; the launch traced here: 34.7 us
  Pallas kernels  34.6 us (99%)
    pallas_call x1, Pallas kernels, exchange_call(): pl.pallas_call(exchange_kernel, out_shape=tuple((jax.ShapeDtypeStruct(sha...  20.8 us
    pallas_call x1, Pallas kernels, step_call(): pl.pallas_call(step_kernel, out_shape=jax.ShapeDtypeStruct(model_state.sh...  13.8 us

profile of v2, /device:TPU:6, one launch (start us, length us, event | category | flops | bytes accessed | tf_op | source)
XLA Modules:
  0.0 34.7 jit_solution(4439356288696660998)
XLA Ops:
  0.0 20.8 %exchange.1 = (s32[2,104,256]{2,1,0:T(8,128)}, f32[96,256]{1,0:T(8,128)}, s32[16,128]{1,0:T(8,128)}, f32[12,24,256]{2,1,0:T(8,128)}, f32[2,40,256]{2,1,0:T(8,128)}, /*index=5*/f32[2,128,128]{2,1,0:T(8,128)}) custom-call(s32[1,1,4]{2,1,0:T(1,128)} %counts.1, f32[1,4,8,128,256]{4,3,2,1,0:T(8,128)} %state.3, s32[1,128,256]{2,1,0:T(8,128)} %mask.3, ...), custom_call_target="tpu_custom_call" | custom-call | tf_op jit(solution)/shard_map/exchange/pallas_call | solution.py:694
  20.8 13.8 %step.1 = f32[1,4,8,128,256]{4,3,2,1,0:T(8,128)} custom-call(f32[1,8]{1,0:T(1,128)} %wave.1, f32[1,8]{1,0:T(1,128)} %spread.1, f32[1,3]{1,0:T(1,128)} %gains.1, f32[1,4,8,128,256]{4,3,2,1,0:T(8,128)} %state.3, s32[1,128,256]{2,1,0:T(8,128)} %mask.3, s32[2,104,256]{2,1,0:T(8,128)} %get-tuple-element.11.places, f32[96,256]{1,0:T(8,128)} %get-tuple-element.12.weights, ...), custom_call_target="tpu_custom_call" | custom-call | tf_op jit(solution)/shard_map/step/pallas_call | solution.py:763

commit v3 on v2

--- a/solution.py
+++ b/solution.py
@@ -14,6 +14,7 @@
 f8 = jnp.float8_e4m3fn
 dma = pltpu.SemaphoreType.DMA
 GROUP = 8
+PICK_UNROLL = 2
 BATCH = 8
 
 
@@ -168,21 +169,6 @@
         def _():
             packet_copy(kind, n, 0, windows).start()
 
-    @pl.when(is_window)
-    def _():
-        pl.semaphore_wait(barrier, 4 + NEAR)
-
-    @pl.when(jnp.logical_and(is_ocean, iy != count_y - 1))
-    def _():
-        pl.semaphore_wait(barrier, 4 + windows * NEAR)
-
-    @pl.when(on_fold)
-    def _():
-        pl.semaphore_wait(barrier, 4 + windows * NEAR + count_x - 1)
-
-    for n in range(NEAR):
-        send_packets("early", n)
-
     loads[2].wait()
     loads[3].wait()
     for at, variable in enumerate((3, 1, 2)):
@@ -195,22 +181,50 @@
     row_ids = lax.broadcasted_iota(jnp.int32, (ROWS, COLS), 0)
     col_ids = lax.broadcasted_iota(jnp.int32, (COLS, COLS), 0)
 
-    def pick(n):
-        def pick_row(row, carry):
-            cell = own_v[n : n + 1, pl.ds(pl.multiple_of(row * COLS, COLS), COLS)]
-            hot = jnp.where(row_ids == (cell >> 8), 1.0, 0.0).astype(jnp.bfloat16)
-            chosen = jnp.dot(
-                surface[...],
-                jnp.concatenate([hot, hot], axis=0),
-                preferred_element_type=jnp.float32,
-            )
-            here = col_ids == (cell & (COLS - 1))
-            for at in range(3):
-                part = jnp.where(here, chosen[at * COLS : (at + 1) * COLS], 0.0)
-                late[n, pl.ds(at * GROUP + row, 1), :] = jnp.sum(part, axis=0, keepdims=True)
+    strip = ROWS // 2
+    lanes = lax.broadcasted_iota(jnp.int32, (strip, 128), 1)
+
+    def pack_strip(at, block):
+        half = slice(at * 128, (at + 1) * 128)
+        band = pl.ds(pl.multiple_of(block * strip, strip), strip)
+        near, pair = (127, 126) if at else (0, 0)
+        packed = jnp.where(
+            lanes == 32,
+            pltpu.roll(sea[band, half].astype(jnp.float32), (32 - near) % 128, 1),
+            0.0,
+        )
+        for level in range(levels):
+            turned = pltpu.roll(fields[0, level, band, half], (2 * level - pair) % 128, 1)
+            packed = jnp.where((lanes >> 1) == level, turned, packed)
+            for variable, first in ((2, 16), (3, 24)):
+                turned = pltpu.roll(
+                    fields[variable, level, band, half], (first + level - near) % 128, 1
+                )
+                packed = jnp.where(lanes == first + level, turned, packed)
+        columns_in[at, band] = packed
+
+    def pick(n, side):
+        def pick_rows(part, carry):
+            if side is not None:
+                pack_strip(side, part)
+            for step in range(GROUP // 2):
+                row = part * (GROUP // 2) + step
+                cell = own_v[n : n + 1, pl.ds(pl.multiple_of(row * COLS, COLS), COLS)]
+                hot = jnp.where(row_ids == (cell >> 8), 1.0, 0.0).astype(jnp.bfloat16)
+                chosen = jnp.dot(
+                    surface[...],
+                    jnp.concatenate([hot, hot], axis=0),
+                    preferred_element_type=jnp.float32,
+                )
+                here = col_ids == (cell & (COLS - 1))
+                for at in range(3):
+                    part_of = jnp.where(here, chosen[at * COLS : (at + 1) * COLS], 0.0)
+                    late[n, pl.ds(at * GROUP + row, 1), :] = jnp.sum(
+                        part_of, axis=0, keepdims=True
+                    )
             return carry
 
-        lax.fori_loop(0, GROUP, pick_row, 0, unroll=8)
+        lax.fori_loop(0, 2, pick_rows, 0, unroll=PICK_UNROLL)
 
     edge_copies = []
     for at, device in enumerate((west, east)):
@@ -249,8 +263,6 @@
     fold_keep = pltpu.make_async_copy(columns_in.at[1], fold_got.at[ix], fold_send.at[0])
 
     def send_edges():
-        loads[4].wait()
-        loads[5].wait()
         for at, (near, far) in enumerate(((0, 1), (ROWS - 1, ROWS - 2))):
             for level in range(levels):
                 for item, (variable, row) in enumerate(((0, near), (0, far), (1, near), (3, near))):
@@ -258,31 +270,6 @@
                         variable, level, row : row + 1, :
                     ]
             rows_in[at, 32:33] = sea[near : near + 1].astype(jnp.float32)
-        lanes = lax.broadcasted_iota(jnp.int32, (ROWS, 128), 1)
-        for at, (near, far) in enumerate(((0, 1), (127, 126))):
-            half = slice(at * 128, (at + 1) * 128)
-            columns_in[at] = jnp.where(
-                lanes == 32,
-                pltpu.roll(sea[:, half].astype(jnp.float32), (32 - near) % 128, 1),
-                0.0,
-            )
-
-            def add_level(level, carry):
-                packed = columns_in[at]
-                for item, (variable, column) in enumerate(
-                    ((0, near), (0, far), (2, near), (3, near))
-                ):
-                    place_at = item * 8 + level
-                    turned = pltpu.roll(
-                        fields[variable, level, :, half],
-                        lax.rem(place_at + (128 - column), 128),
-                        1,
-                    )
-                    packed = jnp.where(lanes == place_at, turned, packed)
-                columns_in[at] = packed
-                return carry
-
-            lax.fori_loop(0, levels, add_level, 0, unroll=2)
         for copy in edge_copies:
             copy.start()
 
@@ -292,12 +279,32 @@
             for step in range(1, count_x):
                 fold_copy(step).start()
 
-    pick(0)
+    pick(3, None)
+    @pl.when(is_window)
+    def _():
+        pl.semaphore_wait(barrier, 4 + NEAR)
+
+    @pl.when(jnp.logical_and(is_ocean, iy != count_y - 1))
+    def _():
+        pl.semaphore_wait(barrier, 4 + windows * NEAR)
+
+    @pl.when(on_fold)
+    def _():
+        pl.semaphore_wait(barrier, 4 + windows * NEAR + count_x - 1)
+
+    for n in reversed(range(NEAR)):
+        send_packets("early", n)
+
+    send_packets("late", 3)
+    loads[4].wait()
+    loads[5].wait()
+    pick(2, 0)
+    send_packets("late", 2)
+    pick(1, 1)
+    send_packets("late", 1)
+    send_edges()
+    pick(0, None)
     send_packets("late", 0)
-    for n in range(1, NEAR):
-        pick(n)
-        send_packets("late", n)
-    send_edges()
 
     def wait_slot(kind, at):
         target_ref, recv, source = {
@@ -401,6 +408,10 @@
                 piece = rest.astype(jnp.bfloat16)
                 rest = rest - piece.astype(f32)
                 gathered += jnp.dot(hot, piece, preferred_element_type=f32)
+        swapped = jnp.where(
+            (lanes & 1) == 0, pltpu.roll(gathered, 127, 1), pltpu.roll(gathered, 1, 1)
+        )
+        gathered = jnp.where(lanes < 16, swapped, gathered)
         turned = jnp.logical_and(lanes >= 16, lanes < 24)
         columns_got[1] = jnp.where(turned, -gathered, gathered)
 
@@ -554,11 +565,18 @@
         edge_rows = [
             [rows_v[side, pl.ds(item * 8 + level, 1), :] for item in range(4)] for side in range(2)
         ]
-        turn = lax.rem(128 - level, 128)
-        shifted = [pltpu.roll(columns_v[side], turn, 1) for side in range(2)]
-        edge_cols = [
-            [shifted[side][:, item * 8 : item * 8 + 1] for item in range(4)] for side in range(2)
-        ]
+        edge_cols = []
+        for side in range(2):
+            pairs = pltpu.roll(columns_v[side], lax.rem(128 - 2 * level, 128), 1)
+            others = pltpu.roll(columns_v[side], lax.rem(128 - level, 128), 1)
+            edge_cols.append(
+                [
+                    pairs[:, 1 - side : 2 - side],
+                    pairs[:, side : side + 1],
+                    others[:, 16:17],
+                    others[:, 24:25],
+                ]
+            )
         row_keep = [
             (1.0 - drag * (1.0 - rows_v[0, 32:33, :])) * valid_west,
             (1.0 - drag * (1.0 - rows_v[1, 32:33, :])) * valid_east,

time: 35 us -> 33.4 us (0.954)
  the two profiles are of different devices: /device:TPU:6 before, /device:TPU:30 now
where the time goes in v3:
time: 33.4 us; the launch traced here: 33.2 us
  Pallas kernels  33.2 us (99%)
    pallas_call x1, Pallas kernels, exchange_call(): pl.pallas_call(exchange_kernel, out_shape=tuple((jax.ShapeDtypeStruct(sha...  17.6 us
    pallas_call x1, Pallas kernels, step_call(): pl.pallas_call(step_kernel, out_shape=jax.ShapeDtypeStruct(model_state.sh...  15.6 us

profile of v3, /device:TPU:30, one launch (start us, length us, event | category | flops | bytes accessed | tf_op | source)
XLA Modules:
  0.0 33.2 jit_solution(8108596634128578422)
XLA Ops:
  0.0 17.6 %exchange.1 = (s32[2,104,256]{2,1,0:T(8,128)}, f32[96,256]{1,0:T(8,128)}, s32[16,128]{1,0:T(8,128)}, f32[12,24,256]{2,1,0:T(8,128)}, f32[2,40,256]{2,1,0:T(8,128)}, /*index=5*/f32[2,128,128]{2,1,0:T(8,128)}) custom-call(s32[1,1,4]{2,1,0:T(1,128)} %counts.1, f32[1,4,8,128,256]{4,3,2,1,0:T(8,128)} %state.3, s32[1,128,256]{2,1,0:T(8,128)} %mask.3, ...), custom_call_target="tpu_custom_call" | custom-call | tf_op jit(solution)/shard_map/exchange/pallas_call | solution.py:712
  17.6 15.6 %step.1 = f32[1,4,8,128,256]{4,3,2,1,0:T(8,128)} custom-call(f32[1,8]{1,0:T(1,128)} %wave.1, f32[1,8]{1,0:T(1,128)} %spread.1, f32[1,3]{1,0:T(1,128)} %gains.1, f32[1,4,8,128,256]{4,3,2,1,0:T(8,128)} %state.3, s32[1,128,256]{2,1,0:T(8,128)} %mask.3, s32[2,104,256]{2,1,0:T(8,128)} %get-tuple-element.11.places, f32[96,256]{1,0:T(8,128)} %get-tuple-element.12.weights, ...), custom_call_target="tpu_custom_call" | custom-call | tf_op jit(solution)/shard_map/step/pallas_call | solution.py:781

commit v4 on v3

--- a/solution.py
+++ b/solution.py
@@ -467,6 +467,12 @@
     def level_load(level):
         return pltpu.make_async_copy(state.at[0, :, level], fields.at[level], level_sem.at[level])
 
+    def first_store(half):
+        span = pl.ds(half * 64, 64)
+        return pltpu.make_async_copy(
+            updated.at[0, :, span], result.at[0, :, 0, span], store_sem.at[half * levels]
+        )
+
     def level_store(level):
         return pltpu.make_async_copy(
             updated.at[level], result.at[0, :, level], store_sem.at[level]
@@ -505,7 +511,7 @@
 
     live_lines = lax.fori_loop(0, jnp.where(is_ocean, packets, NEAR), list_packet, 0)
 
-    for load in loads[1:]:
+    for load in loads[1:3]:
         load.wait()
 
     def split_packets(group, carry):
@@ -524,6 +530,8 @@
         return carry
 
     lax.fori_loop(0, jnp.where(is_ocean, packets // NEAR, 1), split_packets, 0)
+    for load in loads[3:]:
+        load.wait()
     land[...] = 1.0 - sea_v[...].astype(jnp.float32)
     one = jnp.float32(1.0)
     zero = jnp.float32(0.0)
@@ -634,8 +642,8 @@
         tile = jnp.broadcast_to(line, (16, COLS)).astype(kind)
         return jnp.concatenate([tile] * (count // 16), axis=0)
 
-    def scatter(batch):
-        for at in range(BATCH):
+    def scatter(batch, count):
+        for at in range(count):
             line = pl.ds(order[batch * BATCH + at], 1)
             span = slice(at * COLS, (at + 1) * COLS)
             here = narrow_ids == repeated(places_v[0, line, :], 64, jnp.int16)
@@ -649,15 +657,15 @@
             there = wide_ids == repeated(places_v[1, line, :], 2 * COLS, jnp.int16)
             right[:, span] = jnp.where(there, one16, zero16).astype(f8)
         total[...] += lax.dot_general(
-            left[...],
-            right[...],
+            left[:, 0 : count * COLS],
+            right[:, 0 : count * COLS],
             (((1,), (1,)), ((), ())),
             preferred_element_type=jnp.float32,
         )
 
     def level_step(level, carry):
         stencil(level)
-        scatter(level)
+        scatter(level, BATCH)
 
         @pl.when(level > 0)
         def _():
@@ -668,10 +676,17 @@
     lax.fori_loop(0, levels, level_step, 0)
 
     def extra_step(batch, carry):
-        scatter(batch)
+        scatter(batch, BATCH)
         return carry
 
-    lax.fori_loop(levels, jnp.maximum(levels, (live_lines + BATCH - 1) // BATCH), extra_step, 0)
+    batches = levels + jnp.maximum(live_lines - levels * BATCH, 0) // BATCH
+    rest = live_lines - batches * BATCH
+    batches = jnp.where(rest > BATCH // 2, batches + 1, batches)
+    lax.fori_loop(levels, batches, extra_step, 0)
+
+    @pl.when(live_lines > batches * BATCH)
+    def _():
+        scatter(batches, BATCH // 2)
 
     for half in range(2):
         span = slice(half * 64, (half + 1) * 64)
@@ -688,9 +703,11 @@
             updated[0, variable, span] = updated[0, variable, span] + tendency * gain * (
                 sums[item] - sums[3] * fields[0, variable, span]
             )
-    level_store(0).start()
-    for level in range(levels):
+        first_store(half).start()
+    for level in range(1, levels):
         level_store(level).wait()
+    for half in range(2):
+        first_store(half).wait()
 
 
 def exchange_call(
@@ -801,7 +818,7 @@
             pltpu.VMEM((3 * 4 * 64, 2 * COLS), f32),
             dma((7,)),
             dma((levels,)),
-            dma((levels,)),
+            dma((levels + 1,)),
         ],
         compiler_params=pltpu.CompilerParams(vmem_limit_bytes=60 * 2**20),
         name="step",

time: 33.4 us -> 32.2 us (0.964)
  the two profiles are of different devices: /device:TPU:30 before, /device:TPU:6 now
where the time goes in v4:
time: 32.2 us; the launch traced here: 31.8 us
  Pallas kernels  31.8 us (99%)
    pallas_call x1, Pallas kernels, exchange_call(): pl.pallas_call(exchange_kernel, out_shape=tuple((jax.ShapeDtypeStruct(sha...  18.9 us
    pallas_call x1, Pallas kernels, step_call(): pl.pallas_call(step_kernel, out_shape=jax.ShapeDtypeStruct(model_state.sh...  13 us

profile of v4, /device:TPU:6, one launch (start us, length us, event | category | flops | bytes accessed | tf_op | source)
XLA Modules:
  0.0 31.8 jit_solution(13573096563907789209)
XLA Ops:
  0.0 18.9 %exchange.1 = (s32[2,104,256]{2,1,0:T(8,128)}, f32[96,256]{1,0:T(8,128)}, s32[16,128]{1,0:T(8,128)}, f32[12,24,256]{2,1,0:T(8,128)}, f32[2,40,256]{2,1,0:T(8,128)}, /*index=5*/f32[2,128,128]{2,1,0:T(8,128)}) custom-call(s32[1,1,4]{2,1,0:T(1,128)} %counts.1, f32[1,4,8,128,256]{4,3,2,1,0:T(8,128)} %state.3, s32[1,128,256]{2,1,0:T(8,128)} %mask.3, ...), custom_call_target="tpu_custom_call" | custom-call | tf_op jit(solution)/shard_map/exchange/pallas_call | solution.py:729
  18.9 13.0 %step.1 = f32[1,4,8,128,256]{4,3,2,1,0:T(8,128)} custom-call(f32[1,8]{1,0:T(1,128)} %wave.1, f32[1,8]{1,0:T(1,128)} %spread.1, f32[1,3]{1,0:T(1,128)} %gains.1, f32[1,4,8,128,256]{4,3,2,1,0:T(8,128)} %state.3, s32[1,128,256]{2,1,0:T(8,128)} %mask.3, s32[2,104,256]{2,1,0:T(8,128)} %get-tuple-element.11.places, f32[96,256]{1,0:T(8,128)} %get-tuple-element.12.weights, ...), custom_call_target="tpu_custom_call" | custom-call | tf_op jit(solution)/shard_map/step/pallas_call | solution.py:798

commit v5 on v4

--- a/solution.py
+++ b/solution.py
@@ -681,12 +681,14 @@
 
     batches = levels + jnp.maximum(live_lines - levels * BATCH, 0) // BATCH
     rest = live_lines - batches * BATCH
-    batches = jnp.where(rest > BATCH // 2, batches + 1, batches)
+    batches = jnp.where(rest > BATCH - 2, batches + 1, batches)
     lax.fori_loop(levels, batches, extra_step, 0)
-
-    @pl.when(live_lines > batches * BATCH)
-    def _():
-        scatter(batches, BATCH // 2)
+    rest = live_lines - batches * BATCH
+    for count in range(2, BATCH, 2):
+
+        @pl.when(jnp.logical_and(rest > count - 2, rest <= count))
+        def _():
+            scatter(batches, count)
 
     for half in range(2):
         span = slice(half * 64, (half + 1) * 64)

time: 32.2 us -> 31.8 us (0.988)
  Pallas kernels: 31.8 us -> 31.3 us
    pallas_call x1, Pallas kernels: 13 us -> 12.4 us  [step_call(): pl.pallas_call(step_kernel, out_shape=jax.ShapeDtypeStruct(model_state.sh...]
where the time goes in v5:
time: 31.8 us; the launch traced here: 31.3 us
  Pallas kernels  31.3 us (98%)
    pallas_call x1, Pallas kernels, exchange_call(): pl.pallas_call(exchange_kernel, out_shape=tuple((jax.ShapeDtypeStruct(sha...  18.9 us
    pallas_call x1, Pallas kernels, step_call(): pl.pallas_call(step_kernel, out_shape=jax.ShapeDtypeStruct(model_state.sh...  12.4 us

profile of v5, /device:TPU:6, one launch (start us, length us, event | category | flops | bytes accessed | tf_op | source)
XLA Modules:
  0.0 31.3 jit_solution(12888408530036123670)
XLA Ops:
  0.0 18.9 %exchange.1 = (s32[2,104,256]{2,1,0:T(8,128)}, f32[96,256]{1,0:T(8,128)}, s32[16,128]{1,0:T(8,128)}, f32[12,24,256]{2,1,0:T(8,128)}, f32[2,40,256]{2,1,0:T(8,128)}, /*index=5*/f32[2,128,128]{2,1,0:T(8,128)}) custom-call(s32[1,1,4]{2,1,0:T(1,128)} %counts.1, f32[1,4,8,128,256]{4,3,2,1,0:T(8,128)} %state.3, s32[1,128,256]{2,1,0:T(8,128)} %mask.3, ...), custom_call_target="tpu_custom_call" | custom-call | tf_op jit(solution)/shard_map/exchange/pallas_call | solution.py:731
  18.9 12.4 %step.1 = f32[1,4,8,128,256]{4,3,2,1,0:T(8,128)} custom-call(f32[1,8]{1,0:T(1,128)} %wave.1, f32[1,8]{1,0:T(1,128)} %spread.1, f32[1,3]{1,0:T(1,128)} %gains.1, f32[1,4,8,128,256]{4,3,2,1,0:T(8,128)} %state.3, s32[1,128,256]{2,1,0:T(8,128)} %mask.3, s32[2,104,256]{2,1,0:T(8,128)} %get-tuple-element.11.places, f32[96,256]{1,0:T(8,128)} %get-tuple-element.12.weights, ...), custom_call_target="tpu_custom_call" | custom-call | tf_op jit(solution)/shard_map/step/pallas_call | solution.py:800
